TPU v7x, 32 devices: a whole 2x2x4 slice. The times are simulated.
32 devices in a mesh: dp: 4 (over x, core), ctx: 8 (over z, y).
Axes of the slice: x: 2, y: 2, z: 4, core: 2. Of those that a mesh axis runs over, the one named last changes fastest.
Arguments:
- latent: bfloat16 [4, 1024, 576], P('dp', 'ctx'), may hold values from -4 to 4
- query: bfloat16 [4, 1024, 64, 576], P('dp', 'ctx'), may hold values from -24 to 24
- out_grad: bfloat16 [4, 1024, 64, 128], P('dp', 'ctx'), may hold values from -6 to 6
- value_weight: bfloat16 [512, 8192], P('ctx'), may hold values from -0.25 to 0.25
- doc_lengths: int32 [4, 8], P('dp'), may hold values from 1 to 192, 1024 in all within a row
- resumed: int32 [4, 8], P('dp'), may hold values 0 or 1
- groups: int32 [4, 1024], P('dp', 'ctx'), may hold values from 0 to 3, never falling along the last dimension, each value on 1 to 768 neighbouring positions
- reward: float32 [4, 1024], P('dp', 'ctx'), may hold values from -2 to 43.2
Outputs:
- latent_grad: float32 [4, 1024, 576], P('dp', 'ctx')
- value_weight_grad: float32 [512, 8192], P('ctx')
Inputs may be any that keep to these rules, and one draw needn't show every extreme that they name: `doc_lengths`: each sequence's lengths sum to 1024. `groups`: group ids never fall along a sequence, and every id appears in every sequence.
All inputs are finite; a program needn't handle non-finite values. No bound on the sum of `resumed` on one device may be relied on, other than what follows from the above.
Results may differ from a plain program's by a relative error of at most 0.014.
Values may be sent and summed in bfloat16 or wider, within the bound.
A program may use at most 128 MiB of HBM per device.

v0:
```python
import functools

import jax
import jax.numpy as jnp
from jax import lax
from jax.experimental import pallas as pl
from jax.experimental.pallas import tpu as pltpu
from jax.sharding import PartitionSpec as P

LAT = 512
ROPE = 64
NGROUP = 4
HB = 4
BACK = 3
MESH = pl.DeviceIdType.MESH
VMEM = pltpu.VMEM

score_scale = 192.0 ** (-0.5)
LOG2E = 1.4426950408889634


def enter(targets):
    barrier = pltpu.get_barrier_semaphore()
    for target in targets:
        pl.semaphore_signal(barrier, inc=1, device_id=target, device_id_type=MESH)
    pl.semaphore_wait(barrier, len(targets))


def start_kernel(n, docs, lengths, resumed, latent, groups, reward, keys, bias, weight,
                 mine, got, key_send, key_recv, sum_send, sum_recv):
    me = lax.axis_index("ctx")
    rows = latent.shape[0]
    ids = groups[...]
    gains = reward[...]
    for g in range(NGROUP):
        hit = ids == g
        mine[g : g + 1, :] = jnp.where(hit, gains, 0.0)
        mine[NGROUP + g : NGROUP + g + 1, :] = jnp.where(hit, 1.0, 0.0)
    enter([{"ctx": lax.rem(me + d, n)} for d in range(1, n)])
    sends = []
    for d in range(1, n):
        target = {"ctx": lax.rem(me + d, n)}
        sends.append(pltpu.make_async_remote_copy(
            src_ref=mine, dst_ref=got.at[d - 1], send_sem=sum_send.at[d - 1],
            recv_sem=sum_recv.at[d - 1], device_id=target, device_id_type=MESH))
        sends[-1].start()
    moves = []
    for d in range(1, BACK + 1):
        target = {"ctx": lax.rem(me + d, n)}
        moves.append(pltpu.make_async_remote_copy(
            src_ref=latent, dst_ref=keys.at[pl.ds((BACK - d) * rows, rows)],
            send_sem=key_send.at[d - 1], recv_sem=key_recv.at[d - 1],
            device_id=target, device_id_type=MESH))
        moves[-1].start()
    keys[BACK * rows :, :] = latent[...]
    first = me * rows
    query_pos = first + lax.broadcasted_iota(jnp.int32, (1, rows), 1)
    low = jnp.zeros((1, rows), jnp.int32)
    start = jnp.int32(0)
    before = jnp.int32(0)
    for e in range(docs):
        reach = jnp.where(resumed[0, e] == 1, before, start)
        low = jnp.where(query_pos >= start, reach, low)
        before = start
        start = start + lengths[0, e]
    span = (BACK + 1) * rows
    key_pos = first - BACK * rows + lax.broadcasted_iota(jnp.int32, (span, rows), 0)
    seen = (key_pos >= low) & (key_pos <= query_pos)
    bias[...] = jnp.where(seen, 0.0, -jnp.inf)
    for copy in sends:
        copy.wait()
    total = mine[...]
    for d in range(n - 1):
        total = total + got[d]
    sums = jnp.sum(total, axis=1, keepdims=True)
    mean = jnp.zeros((1, rows), jnp.float32)
    for g in range(NGROUP):
        mean = jnp.where(ids == g, sums[g : g + 1] / sums[NGROUP + g : NGROUP + g + 1], mean)
    token = 0.125 * (gains - mean)
    weight[...] = jnp.transpose(jnp.broadcast_to(token, (rows, rows)))
    for copy in moves:
        copy.wait()


def start_call(n, lengths, resumed, latent, groups, reward):
    rows, width = latent.shape
    span = (BACK + 1) * rows
    vm = pl.BlockSpec(memory_space=VMEM)
    sm = pl.BlockSpec(memory_space=pltpu.SMEM)
    return pl.pallas_call(
        functools.partial(start_kernel, n, lengths.shape[1]),
        out_shape=(
            jax.ShapeDtypeStruct((span, width), jnp.bfloat16),
            jax.ShapeDtypeStruct((span, rows), jnp.float32),
            jax.ShapeDtypeStruct((rows, rows), jnp.float32),
        ),
        in_specs=[sm, sm, vm, vm, vm],
        out_specs=(vm, vm, vm),
        scratch_shapes=[
            VMEM((2 * NGROUP, rows), jnp.float32),
            VMEM((n - 1, 2 * NGROUP, rows), jnp.float32),
            pltpu.SemaphoreType.DMA((BACK,)),
            pltpu.SemaphoreType.DMA((BACK,)),
            pltpu.SemaphoreType.DMA((n - 1,)),
            pltpu.SemaphoreType.DMA((n - 1,)),
        ],
        compiler_params=pltpu.CompilerParams(
            collective_id=0, has_side_effects=True, vmem_limit_bytes=16 << 20),
        cost_estimate=pl.CostEstimate(flops=1 << 20, bytes_accessed=2 << 20, transcendentals=0),
    )(lengths, resumed, latent, groups, reward)


def nt(a, b):
    return lax.dot_general(a, b, (((1,), (1,)), ((), ())), preferred_element_type=jnp.float32)


def nn(a, b):
    return jnp.dot(a, b, preferred_element_type=jnp.float32)


def forward_kernel(with_sum, off, query, grad, keys, values_t, bias, weight, *rest):
    if with_sum:
        partner, prob_ref, term_ref = rest
    else:
        prob_ref, term_ref = rest
    rows = query.shape[1]
    q = query[...].reshape(HB * rows, query.shape[2])
    score = nt(keys[...], q) * (score_scale * LOG2E) + jnp.concatenate([bias[...]] * HB, axis=1)
    peak = jnp.max(score, axis=0, keepdims=True)
    exponent = jnp.exp2(score - peak)
    prob = (exponent * (1.0 / jnp.sum(exponent, axis=0, keepdims=True))).astype(jnp.bfloat16)
    prob_ref[...] = prob
    attended = nn(values_t[...], prob).astype(jnp.bfloat16)
    vdim = grad.shape[2]
    for h in range(HB):
        scaled = (weight[...] * grad[h].astype(jnp.float32)).astype(jnp.bfloat16)
        term = nn(attended[:, h * rows : (h + 1) * rows], scaled)
        part = slice(h * vdim, (h + 1) * vdim)
        if with_sum:
            term = term + partner[:, part].astype(jnp.float32)
        term_ref[:, part] = term.astype(jnp.bfloat16)


def forward_call(off, heads, query, grad, keys, values_t, bias, weight, partner=None):
    rows, width = query.shape[1:]
    vdim = grad.shape[2]
    span = keys.shape[0]
    whole = lambda shape: pl.BlockSpec(shape, lambda i, o: (0, 0))
    by_head = lambda shape: pl.BlockSpec(shape, lambda i, o: (o[0] + i, 0, 0))
    column = lambda height, wide: pl.BlockSpec((height, wide), lambda i, o: (0, i))
    in_specs = [
        by_head((HB, rows, width)), by_head((HB, rows, vdim)), whole((span, width)),
        whole((LAT, span)), whole((span, rows)), whole((rows, rows)),
    ]
    args = [query, grad, keys, values_t, bias, weight]
    if partner is not None:
        in_specs.append(column(LAT, HB * vdim))
        args.append(partner)
    flops = 2 * heads * rows * (span * (width + LAT) + LAT * vdim)
    return pl.pallas_call(
        functools.partial(forward_kernel, partner is not None),
        grid_spec=pltpu.PrefetchScalarGridSpec(
            num_scalar_prefetch=1,
            grid=(heads // HB,),
            in_specs=in_specs,
            out_specs=[column(span, HB * rows), column(LAT, HB * vdim)],
        ),
        out_shape=[
            jax.ShapeDtypeStruct((span, heads * rows), jnp.bfloat16),
            jax.ShapeDtypeStruct((LAT, heads * vdim), jnp.bfloat16),
        ],
        compiler_params=pltpu.CompilerParams(vmem_limit_bytes=48 << 20),
        cost_estimate=pl.CostEstimate(
            flops=flops, bytes_accessed=heads * rows * 4 * (width + span), transcendentals=0),
    )(off, *args)


def backward_kernel(off, query, grad, value_weight, prob_ref, keys, weight, out):
    rows = query.shape[1]
    vdim = grad.shape[2]
    q = query[...].reshape(HB * rows, query.shape[2])
    parts = []
    for h in range(HB):
        scaled = (weight[...] * grad[h].astype(jnp.float32)).astype(jnp.bfloat16)
        parts.append(nt(scaled, value_weight[:, h * vdim : (h + 1) * vdim]).astype(jnp.bfloat16))
    latent_out = jnp.concatenate(parts, axis=0)
    prob_b = prob_ref[...]
    prob = prob_b.astype(jnp.float32)
    prob_grad = nt(keys[:, :LAT], latent_out)
    row_dot = jnp.sum(prob * prob_grad, axis=0, keepdims=True)
    score_grad = (score_scale * prob * (prob_grad - row_dot)).astype(jnp.bfloat16)
    key_part = nn(score_grad, q)
    value_part = nn(prob_b, latent_out)

    @pl.when(pl.program_id(0) == 0)
    def _():
        out[...] = jnp.zeros_like(out)

    out[:, :LAT] += key_part[:, :LAT] + value_part
    out[:, LAT:] += key_part[:, LAT:]


def backward_call(off, heads, query, grad, value_weight, prob, keys, weight):
    rows, width = query.shape[1:]
    vdim = grad.shape[2]
    span = keys.shape[0]
    whole = lambda shape: pl.BlockSpec(shape, lambda i, o: (0, 0))
    by_head = lambda shape: pl.BlockSpec(shape, lambda i, o: (o[0] + i, 0, 0))
    column = lambda height, wide: pl.BlockSpec((height, wide), lambda i, o: (0, i))
    flops = 2 * heads * rows * (span * (width + 2 * LAT) + LAT * vdim)
    return pl.pallas_call(
        backward_kernel,
        grid_spec=pltpu.PrefetchScalarGridSpec(
            num_scalar_prefetch=1,
            grid=(heads // HB,),
            in_specs=[
                by_head((HB, rows, width)), by_head((HB, rows, vdim)), column(LAT, HB * vdim),
                column(span, HB * rows), whole((span, width)), whole((rows, rows)),
            ],
            out_specs=whole((span, width)),
        ),
        out_shape=jax.ShapeDtypeStruct((span, width), jnp.float32),
        compiler_params=pltpu.CompilerParams(vmem_limit_bytes=48 << 20),
        cost_estimate=pl.CostEstimate(
            flops=flops, bytes_accessed=heads * rows * 4 * (width + span), transcendentals=0),
    )(off, query, grad, value_weight, prob, keys, weight)


def key_kernel(n, first, second, out, term, got, send, recv):
    me = lax.axis_index("ctx")
    rows = out.shape[0]
    term[...] = (first[...] + second[...]).astype(jnp.bfloat16)
    enter([{"ctx": lax.rem(me + d, n)} for d in range(1, BACK + 1)]
          + [{"ctx": lax.rem(me + n - d, n)} for d in range(1, BACK + 1)])
    moves = []
    for d in range(1, BACK + 1):
        moves.append(pltpu.make_async_remote_copy(
            src_ref=term.at[pl.ds((BACK - d) * rows, rows)], dst_ref=got.at[d - 1],
            send_sem=send.at[d - 1], recv_sem=recv.at[d - 1],
            device_id={"ctx": lax.rem(me + n - d, n)}, device_id_type=MESH))
        moves[-1].start()
    total = term[BACK * rows :, :].astype(jnp.float32)
    for d in range(1, BACK + 1):
        moves[d - 1].wait()
        total = total + jnp.where(me + d < n, got[d - 1].astype(jnp.float32), 0.0)
    out[...] = total


def key_call(n, first, second):
    span, width = first.shape
    rows = span // (BACK + 1)
    vm = pl.BlockSpec(memory_space=VMEM)
    return pl.pallas_call(
        functools.partial(key_kernel, n),
        out_shape=jax.ShapeDtypeStruct((rows, width), jnp.float32),
        in_specs=[vm, vm],
        out_specs=vm,
        scratch_shapes=[
            VMEM((span, width), jnp.bfloat16),
            VMEM((BACK, rows, width), jnp.bfloat16),
            pltpu.SemaphoreType.DMA((BACK,)),
            pltpu.SemaphoreType.DMA((BACK,)),
        ],
        compiler_params=pltpu.CompilerParams(
            collective_id=1, has_side_effects=True, vmem_limit_bytes=24 << 20),
        cost_estimate=pl.CostEstimate(flops=1 << 20, bytes_accessed=3 << 20, transcendentals=0),
    )(first, second)


def finish_kernel(m, count, *refs):
    parts, (out, across, mine, other, x_send, x_recv, c_send, c_recv) = refs[:count], refs[count:]
    me = lax.axis_index("dp")
    core = lax.rem(me, 2)
    chip = me // 2
    chips = m // 2
    wide = parts[0].shape[1]
    half = wide * count
    partner = {"dp": chip * 2 + (1 - core)}
    peers = [{"dp": lax.rem(chip + d, chips) * 2 + core} for d in range(1, chips)]
    enter(peers + [partner])
    moves = []
    for j in range(count):
        row = []
        for d in range(1, chips):
            row.append(pltpu.make_async_remote_copy(
                src_ref=parts[j], dst_ref=across.at[j, chip],
                send_sem=x_send.at[j, d - 1], recv_sem=x_recv.at[j, d - 1],
                device_id=peers[d - 1], device_id_type=MESH))
            row[-1].start()
        moves.append(row)
    swaps = []
    for j in range(count):
        across[j, chip] = parts[j][...]
        for copy in moves[j]:
            copy.wait()
        total = across[j, 0].astype(jnp.float32)
        for k in range(1, chips):
            total = total + across[j, k].astype(jnp.float32)
        rounded = total.astype(jnp.bfloat16)
        mine[j] = rounded
        swaps.append(pltpu.make_async_remote_copy(
            src_ref=mine.at[j], dst_ref=other.at[j], send_sem=c_send.at[j],
            recv_sem=c_recv.at[j], device_id=partner, device_id_type=MESH))
        swaps[-1].start()
        out[:, pl.ds(pl.multiple_of(core * half + j * wide, 128), wide)] = rounded.astype(jnp.float32)
    for j in range(count):
        swaps[j].wait()
        out[:, pl.ds(pl.multiple_of((1 - core) * half + j * wide, 128), wide)] = (
            other[j].astype(jnp.float32))


def finish_call(m, parts):
    count = len(parts)
    rows, wide = parts[0].shape
    vm = pl.BlockSpec(memory_space=VMEM)
    chips = m // 2
    return pl.pallas_call(
        functools.partial(finish_kernel, m, count),
        out_shape=jax.ShapeDtypeStruct((rows, 2 * wide * count), jnp.float32),
        in_specs=[vm] * count,
        out_specs=vm,
        scratch_shapes=[
            VMEM((count, chips, rows, wide), jnp.bfloat16),
            VMEM((count, rows, wide), jnp.bfloat16),
            VMEM((count, rows, wide), jnp.bfloat16),
            pltpu.SemaphoreType.DMA((count, chips - 1)),
            pltpu.SemaphoreType.DMA((count, chips - 1)),
            pltpu.SemaphoreType.DMA((count,)),
            pltpu.SemaphoreType.DMA((count,)),
        ],
        compiler_params=pltpu.CompilerParams(
            collective_id=2, has_side_effects=True, vmem_limit_bytes=24 << 20),
        cost_estimate=pl.CostEstimate(flops=1 << 20, bytes_accessed=6 << 20, transcendentals=0),
    )(*parts)


CHUNKS = 2


def per_device(latent, query, out_grad, value_weight, doc_lengths, resumed, groups, reward):
    n = lax.axis_size("ctx")
    m = lax.axis_size("dp")
    core = lax.rem(lax.axis_index("dp"), 2)
    heads = query.shape[2]
    half = heads // 2
    quarter = half // CHUNKS
    vdim = out_grad.shape[3]
    swap = [(i, i ^ 1) for i in range(m)]
    half_rows = lax.dynamic_slice_in_dim(value_weight, core * half * vdim, half * vdim, 1)
    own_weight = lax.all_gather(half_rows, "ctx", axis=0, tiled=True)
    keys, bias, weight = start_call(n, doc_lengths, resumed, latent[0], groups, reward)
    values_t = keys[:, :LAT].T
    q = jnp.transpose(query[0], (1, 0, 2))
    grad = jnp.transpose(out_grad[0], (1, 0, 2))
    own_at = [((core * half + j * quarter) // HB).astype(jnp.int32).reshape(1) for j in range(CHUNKS)]
    other_at = [(((1 - core) * half + j * quarter) // HB).astype(jnp.int32).reshape(1)
                for j in range(CHUNKS)]
    other_prob, own_prob, arrived, sums = [], [], [], []
    for j in range(CHUNKS):
        prob, term = forward_call(other_at[j], quarter, q, grad, keys, values_t, bias, weight)
        other_prob.append(prob)
        arrived.append(lax.ppermute(term, "dp", swap))
    for j in range(CHUNKS):
        prob, term = forward_call(
            own_at[j], quarter, q, grad, keys, values_t, bias, weight, arrived[j])
        own_prob.append(prob)
        sums.append(lax.psum_scatter(term, "ctx", scatter_dimension=0, tiled=True))
    other_weight = lax.ppermute(own_weight, "dp", swap)
    pieces = []
    for at, weights, probs in ((own_at, own_weight, own_prob), (other_at, other_weight, other_prob)):
        for j in range(CHUNKS):
            pieces.append(backward_call(
                at[j], quarter, q, grad, weights[:, j * quarter * vdim : (j + 1) * quarter * vdim],
                probs[j], keys, weight))
    first = sum(pieces[1 : len(pieces) // 2], pieces[0])
    second = sum(pieces[len(pieces) // 2 + 1 :], pieces[len(pieces) // 2])
    latent_grad = key_call(n, first, second)
    weight_grad = finish_call(m, sums)
    return (latent_grad[None], weight_grad)


def solution(mesh):
    return jax.shard_map(
        per_device,
        mesh=mesh,
        in_specs=(
            P("dp", "ctx", None),
            P("dp", "ctx", None, None),
            P("dp", "ctx", None, None),
            P("ctx", None),
            P("dp", None),
            P("dp", None),
            P("dp", "ctx"),
            P("dp", "ctx"),
        ),
        out_specs=(P("dp", "ctx", None), P("ctx", None)),
        check_vma=False,
    )
```

profile of v0, /device:TPU:5, one launch (start us, length us, event | category | flops | bytes accessed | tf_op | source)
XLA Modules:
  0.0 323.3 jit_solution(15703971741850434223)
XLA Ops:
  7.2 0.0 copy-start
  7.2 0.0 all-gather.2.cloned.1.call-start
  7.2 1.2 copy-done
  8.4 0.8 constant_dynamic-slice_fusion
  9.2 0.0 all-gather.2.cloned.1.call-update
  9.3 0.0 reduce-scatter.5.cloned.1.call-start
  9.3 1.1 copy.12
  10.4 0.0 copy-start.11
  10.4 0.6 copy-done.11
  11.0 0.0 copy-start.12
  11.0 0.7 copy-done.12
  11.7 0.0 copy-start.13
  11.7 0.7 copy-done.13
  12.4 0.0 copy-start.14
  12.4 0.7 copy-done.14
  13.0 20.9 %shard_map.95 = (bf16[512,576]{1,0:T(8,128)(2,1)S(1)}, f32[512,128]{1,0:T(8,128)S(1)}, f32[128,128]{1,0:T(8,128)S(1)}) custom-call(s32[1,8]{1,0:T(1,128)S(1)} %copy-done.11, s32[1,8]{1,0:T(1,128)S(1)} %copy-done.12, bf16[128,576]{1,0:T(8,128)(2,1)S(1)} %bitcast.25, s32[1,128]{1,0:T(1,128)S(1)} %copy-done.13, f32[1,128]{1,0:T(1,128)S(1)} %copy-done.14), custom_call_target="tpu_custom_call" | custom-call | flops 1048576 | bytes 2097152 | tf_op jit(solution)/shard_map/pallas_call | solution.py:90
  33.9 0.2 copy.13
  34.2 4.3 %copy.16 = bf16[1,128,64,128]{3,1,2,0:T(8,128)(2,1)} copy(bf16[1,128,64,128]{3,2,1,0:T(8,128)(2,1)} %param.10) | data formatting | bytes 4194304 | tf_op args[2]
  38.4 14.0 %copy.10 = bf16[1,128,64,576]{3,1,2,0:T(8,128)(2,1)} copy(bf16[1,128,64,576]{1,3,2,0:T(8,128)(2,1)} %param.9) | data formatting | bytes 18874368 | tf_op args[1]
  52.5 7.8 %shard_map.99 = (bf16[512,2048]{1,0:T(8,128)(2,1)S(1)}, bf16[512,2048]{1,0:T(8,128)(2,1)}) custom-call(s32[1]{0:T(128)} %bitcast.11.off, bf16[64,128,576]{2,1,0:T(8,128)(2,1)} %bitcast.26, bf16[64,128,128]{2,1,0:T(8,128)(2,1)} %bitcast.16, bf16[512,576]{1,0:T(8,128)(2,1)S(1)} %get-tuple-element.13.keys, bf16[512,512]{1,0:T(8,128)(2,1)S(1)} %slice_bitcast_fusion.values_t, ...), custom_call_target="tpu_custom_call" | custom-call | flops 2550136832 | bytes 8912896 | tf_op jit(solution)/shard_map/pallas_call | solution.py:160
  60.3 0.0 copy-start.5
  60.3 1.3 copy-done.5
  61.6 3.8 %collective-permute-start.1 = (bf16[512,2048]{1,0:T(8,128)(2,1)}, bf16[512,2048]{1,0:T(8,128)(2,1)}, u32[]{:S(2)}, u32[]{:S(2)}) collective-permute-start(bf16[512,2048]{1,0:T(8,128)(2,1)} %get-tuple-element.18), channel_id=1, source_target_pairs={{0,8},{8,0},{16,24},{24,16},{1,9},{9,1},{17,25},{25,17},{2,10},{10... | collective-permute-start | bytes 6291464 | tf_op jit(solution)/shard_map/ppermute | solution.py:362
  65.4 4.1 %collective-permute-done.1.rest_0_ = bf16[512,2048]{1,0:T(8,128)(2,1)} collective-permute-done((bf16[512,2048]{1,0:T(8,128)(2,1)}, bf16[512,2048]{1,0:T(8,128)(2,1)}, u32[]{:S(2)}, u32[]{:S(2)}) %collective-permute-start.1) | collective-permute-done | bytes 2097184 | tf_op jit(solution)/shard_map/ppermute | solution.py:362
  69.6 7.4 %shard_map.100 = (bf16[512,2048]{1,0:T(8,128)(2,1)S(1)}, bf16[512,2048]{1,0:T(8,128)(2,1)S(1)}) custom-call(s32[1]{0:T(128)} %bitcast.10.off, bf16[64,128,576]{2,1,0:T(8,128)(2,1)} %bitcast.27, bf16[64,128,128]{2,1,0:T(8,128)(2,1)} %bitcast.17, bf16[512,576]{1,0:T(8,128)(2,1)S(1)} %get-tuple-element.13.keys, ...), custom_call_target="tpu_custom_call" | custom-call | flops 2550136832 | bytes 8912896 | tf_op jit(solution)/shard_map/pallas_call | solution.py:160
  76.9 0.0 copy-start.3
  77.0 1.4 copy-done.3
  78.3 0.0 copy-start.6
  78.3 1.4 copy-done.6
  79.7 0.0 reduce-scatter.5.cloned.1.call-update
  79.8 0.2 reduce-scatter.3.cloned.1.call-start
  80.0 7.9 %shard_map.96 = (bf16[512,2048]{1,0:T(8,128)(2,1)S(1)}, bf16[512,2048]{1,0:T(8,128)(2,1)}) custom-call(s32[1]{0:T(128)} %bitcast.9.off, bf16[64,128,576]{2,1,0:T(8,128)(2,1)} %bitcast.28, bf16[64,128,128]{2,1,0:T(8,128)(2,1)} %bitcast.18, bf16[512,576]{1,0:T(8,128)(2,1)S(1)} %get-tuple-element.13.keys, bf16[512,512]{1,0:T(8,128)(2,1)S(1)} %slice_bitcast_fusion.values_t, ...), custom_call_target="tpu_custom_call" | custom-call | flops 2550136832 | bytes 8912896 | tf_op jit(solution)/shard_map/pallas_call | solution.py:160
  87.9 0.0 copy-start.7
  87.9 1.3 copy-done.7
  89.3 0.4 collective-permute-start
  89.6 4.1 %collective-permute-done.rest_0_ = bf16[512,2048]{1,0:T(8,128)(2,1)} collective-permute-done((bf16[512,2048]{1,0:T(8,128)(2,1)}, bf16[512,2048]{1,0:T(8,128)(2,1)}, u32[]{:S(2)}, u32[]{:S(2)}) %collective-permute-start) | collective-permute-done | bytes 2097184 | tf_op jit(solution)/shard_map/ppermute | solution.py:362
  93.8 7.4 %shard_map.97 = (bf16[512,2048]{1,0:T(8,128)(2,1)S(1)}, bf16[512,2048]{1,0:T(8,128)(2,1)S(1)}) custom-call(s32[1]{0:T(128)} %bitcast.off, bf16[64,128,576]{2,1,0:T(8,128)(2,1)} %bitcast.29, bf16[64,128,128]{2,1,0:T(8,128)(2,1)} %bitcast.19, bf16[512,576]{1,0:T(8,128)(2,1)S(1)} %get-tuple-element.13.keys, bf16[512,512]{1,0:T(8,128)(2,1)S(1)} %slice_bitcast_fusion.values_t, ...), custom_call_target="tpu_custom_call" | custom-call | flops 2550136832 | bytes 8912896 | tf_op jit(solution)/shard_map/pallas_call | solution.py:160
  101.2 0.0 copy-start.4
  101.2 1.3 copy-done.4
  102.5 1.3 copy-done.8
  103.8 0.0 reduce-scatter.3.cloned.1.call-update
  103.8 0.0 all-gather.2.cloned.1.call-done
  103.9 0.4 collective-permute-start.2
  104.3 59.0 %reduce-scatter.5.cloned.1.call-done.refs_1_ = bf16[64,2048]{1,0:T(8,128)(2,1)} async-done(((bf16[512,2048]{1,0:T(8,128)(2,1)}), bf16[64,2048]{1,0:T(8,128)(2,1)}) %reduce-scatter.5.cloned.1.call-update) | async-done | bytes 262160 | tf_op jit(solution)/shard_map/reduce_scatter | solution.py:367
  163.3 70.2 %reduce-scatter.3.cloned.1.call-done.refs_0_ = bf16[64,2048]{1,0:T(8,128)(2,1)} async-done(((bf16[512,2048]{1,0:T(8,128)(2,1)}), bf16[64,2048]{1,0:T(8,128)(2,1)}) %reduce-scatter.3.cloned.1.call-update) | async-done | bytes 262160 | tf_op jit(solution)/shard_map/reduce_scatter | solution.py:367
  233.5 0.9 copy-done.9
  234.5 0.9 copy-done.10
  235.4 17.1 %shard_map.105 = f32[64,8192]{1,0:T(8,128)S(1)} custom-call(bf16[64,2048]{1,0:T(8,128)(2,1)S(1)} %copy-done.10, bf16[64,2048]{1,0:T(8,128)(2,1)S(1)} %copy-done.9), custom_call_target="tpu_custom_call" | custom-call | flops 1048576 | bytes 6291456 | tf_op jit(solution)/shard_map/pallas_call | solution.py:317
  252.5 0.0 copy-start.2
  252.5 5.0 %fusion.1 = (bf16[512,2048]{1,0:T(8,128)(2,1)}, bf16[512,2048]{1,0:T(8,128)(2,1)}) fusion(bf16[512,4096]{1,0:T(8,128)(2,1)} %all-gather.2.cloned.1.call-done), kind=kLoop, calls=%fused_computation.4 | loop fusion | bytes 8388608 | tf_op jit(solution)/shard_map/slice | solution.py:373
  257.5 0.0 copy-done.2
  257.5 8.4 %shard_map.101 = f32[512,576]{1,0:T(8,128)S(1)} custom-call(s32[1]{0:T(128)} %bitcast.10.off, bf16[64,128,576]{2,1,0:T(8,128)(2,1)} %bitcast.30, bf16[64,128,128]{2,1,0:T(8,128)(2,1)S(1)} %bitcast.20, bf16[512,2048]{1,0:T(8,128)(2,1)} %get-tuple-element.28.value_weight, bf16[512,2048]{1,0:T(8,128)(2,1)} %copy-done.6, ...), custom_call_target="tpu_custom_call" | custom-call | flops 3623878656 | bytes 8912896 | tf_op jit(solution)/shard_map/pallas_call | solution.py:211
  265.9 8.4 %shard_map.98 = f32[512,576]{1,0:T(8,128)S(1)} custom-call(s32[1]{0:T(128)} %bitcast.off, bf16[64,128,576]{2,1,0:T(8,128)(2,1)} %bitcast.31, bf16[64,128,128]{2,1,0:T(8,128)(2,1)S(1)} %bitcast.21, bf16[512,2048]{1,0:T(8,128)(2,1)} %get-tuple-element.29.value_weight, bf16[512,2048]{1,0:T(8,128)(2,1)} %copy-done.8, ...), custom_call_target="tpu_custom_call" | custom-call | flops 3623878656 | bytes 8912896 | tf_op jit(solution)/shard_map/pallas_call | solution.py:211
  274.3 0.1 add.26.first
  274.4 0.0 collective-permute-done.2
  274.4 4.8 %fusion = (bf16[512,2048]{1,0:T(8,128)(2,1)}, bf16[512,2048]{1,0:T(8,128)(2,1)}) fusion(bf16[512,4096]{1,0:T(8,128)(2,1)} %collective-permute-done.2), kind=kLoop, calls=%fused_computation.3 | loop fusion | bytes 8388608 | tf_op jit(solution)/shard_map/slice | solution.py:373
  279.3 8.4 %shard_map.103 = f32[512,576]{1,0:T(8,128)S(1)} custom-call(s32[1]{0:T(128)} %bitcast.11.off, bf16[64,128,576]{2,1,0:T(8,128)(2,1)} %bitcast.32, bf16[64,128,128]{2,1,0:T(8,128)(2,1)S(1)} %bitcast.22, bf16[512,2048]{1,0:T(8,128)(2,1)} %get-tuple-element.26.value_weight, bf16[512,2048]{1,0:T(8,128)(2,1)} %copy-done.5, ...), custom_call_target="tpu_custom_call" | custom-call | flops 3623878656 | bytes 8912896 | tf_op jit(solution)/shard_map/pallas_call | solution.py:211
  287.6 8.4 %shard_map.102 = f32[512,576]{1,0:T(8,128)S(1)} custom-call(s32[1]{0:T(128)} %bitcast.9.off, bf16[64,128,576]{2,1,0:T(8,128)(2,1)} %bitcast.33, bf16[64,128,128]{2,1,0:T(8,128)(2,1)S(1)} %bitcast.23, bf16[512,2048]{1,0:T(8,128)(2,1)} %get-tuple-element.27.value_weight, bf16[512,2048]{1,0:T(8,128)(2,1)} %copy-done.7, ...), custom_call_target="tpu_custom_call" | custom-call | flops 3623878656 | bytes 8912896 | tf_op jit(solution)/shard_map/pallas_call | solution.py:211
  296.0 0.1 add.27.second
  296.1 18.4 %shard_map.104 = f32[128,576]{1,0:T(8,128)S(1)} custom-call(f32[512,576]{1,0:T(8,128)S(1)} %add.26.first, f32[512,576]{1,0:T(8,128)S(1)} %add.27.second), custom_call_target="tpu_custom_call" | custom-call | flops 1048576 | bytes 3145728 | tf_op jit(solution)/shard_map/pallas_call | solution.py:253
  314.6 0.0 copy-start.1
  314.6 0.9 copy.14
  315.5 1.3 copy.18
  316.8 0.0 copy-done.1
  (4 shorter events, 0.0 us)
Async XLA Ops:
  7.2 1.2 copy-start
  7.2 96.7 %all-gather.2.cloned.1.call-start = ((), (), s32[]{:S(2)}) async-start(), calls=%async_computation.2 | async-start | bytes 4718592 | tf_op jit(solution)/shard_map/all_gather | solution.py:350
  9.3 154.1 %reduce-scatter.5.cloned.1.call-start = ((), (), s32[]{:S(2)}) async-start(), calls=%async_computation.4 | async-start | bytes 2359296 | tf_op jit(solution)/shard_map/reduce_scatter | solution.py:367
  10.4 0.7 copy-start.11
  11.0 0.7 copy-start.12
  11.7 0.7 copy-start.13
  12.4 0.7 copy-start.14
  60.3 1.3 copy-start.5
  61.6 7.9 %collective-permute-start.1 = (bf16[512,2048]{1,0:T(8,128)(2,1)}, bf16[512,2048]{1,0:T(8,128)(2,1)}, u32[]{:S(2)}, u32[]{:S(2)}) collective-permute-start(bf16[512,2048]{1,0:T(8,128)(2,1)} %get-tuple-element.18), channel_id=1, source_target_pairs={{0,8},{8,0},{16,24},{24,16},{1,9},{9,1},{17,25},{25,17},{2,10},{10... | collective-permute-start | bytes 6291464 | tf_op jit(solution)/shard_map/ppermute | solution.py:362
  76.9 1.4 copy-start.3
  78.3 1.4 copy-start.6
  79.8 153.8 %reduce-scatter.3.cloned.1.call-start = ((), (), s32[]{:S(2)}) async-start(), calls=%async_computation.3 | async-start | bytes 2359296 | tf_op jit(solution)/shard_map/reduce_scatter | solution.py:367
  87.9 1.3 copy-start.7
  89.3 4.5 %collective-permute-start = (bf16[512,2048]{1,0:T(8,128)(2,1)}, bf16[512,2048]{1,0:T(8,128)(2,1)}, u32[]{:S(2)}, u32[]{:S(2)}) collective-permute-start(bf16[512,2048]{1,0:T(8,128)(2,1)} %get-tuple-element.16), channel_id=1, source_target_pairs={{0,8},{8,0},{16,24},{24,16},{1,9},{9,1},{17,25},{25,17},{2,10},{10... | collective-permute-start | bytes 6291464 | tf_op jit(solution)/shard_map/ppermute | solution.py:362
  101.2 1.3 copy-start.4
  102.5 1.3 copy-start.8
  103.9 170.5 %collective-permute-start.2 = (bf16[512,4096]{1,0:T(8,128)(2,1)}, bf16[512,4096]{1,0:T(8,128)(2,1)}, u32[]{:S(2)}, u32[]{:S(2)}) collective-permute-start(bf16[512,4096]{1,0:T(8,128)(2,1)} %all-gather.2.cloned.1.call-done), channel_id=1, source_target_pairs={{0,8},{8,0},{16,24},{24,16},{1,9},{9,1},{17,25},{25,17},{2,10},{10... | collective-permute-start | bytes 12582920 | tf_op jit(solution)/shard_map/ppermute | solution.py:368
  233.5 0.9 copy-start.9
  234.5 0.9 copy-start.10
  252.5 5.0 %copy-start.2 = (bf16[1,128,64,128]{3,1,2,0:T(8,128)(2,1)S(1)}, bf16[1,128,64,128]{3,1,2,0:T(8,128)(2,1)}, u32[]{:S(2)}) copy-start(bf16[1,128,64,128]{3,1,2,0:T(8,128)(2,1)} %copy.16) | copy-start | bytes 6291460
  314.6 2.2 copy-start.1
Sparse Core Ops, SparseCore 0:
  10.1 82.9 all-gather.1
  96.7 66.6 reduce-scatter.4
  166.9 66.6 reduce-scatter.2
where the time goes:
time: 324 us; the launch traced here: 323 us
  waiting for transfers between devices  138 us (43%)
  Pallas kernels  120 us (37%)
  local copies, waits for them, and re-layouts  46.3 us (14%)
  between operations  14 us (4%)
  starting transfers between devices  4.93 us (2%)
    reduce_scatter x2, waiting for transfers between devices, per_device(): sums.append(lax.psum_scatter(term, 'ctx', scatter_dimension=0, tiled=True))  129 us
    unnamed x35, local copies, waits for them, and re-layouts  35.3 us
    pallas_call x4, Pallas kernels, backward_call(): pl.pallas_call(backward_kernel, grid_spec=pltpu.PrefetchScalarGridSpec(nu...  33.4 us
    pallas_call x4, Pallas kernels, forward_call(): pl.pallas_call(functools.partial(forward_kernel, partner is not None), gr...  30.5 us
    pallas_call x1, Pallas kernels, start_call(): pl.pallas_call(functools.partial(start_kernel, n, lengths.shape[1]), out_...  20.9 us
    pallas_call x1, Pallas kernels, key_call(): pl.pallas_call(functools.partial(key_kernel, n), out_shape=jax.ShapeDtype...  18.4 us
    pallas_call x1, Pallas kernels, finish_call(): pl.pallas_call(functools.partial(finish_kernel, m, count), out_shape=jax....  17.1 us
    slice x2, local copies, waits for them, and re-layouts, per_device(): weights[:, j * quarter * vdim:(j + 1) * quarter * vdim]  9.86 us
  transfers between devices with their start and end apart: 6, of which 4 were waited for; matrix products, arithmetic and copies ran while one was open for 8% of the time, Pallas kernels for 26%

commit v1 on v0

--- a/solution.py
+++ b/solution.py
@@ -120,12 +120,13 @@
 
 def forward_kernel(with_sum, off, query, grad, keys, values_t, bias, weight, *rest):
     if with_sum:
-        partner, prob_ref, term_ref = rest
+        partner, prob_ref, away_ref, kept_ref = rest
+        middle = away_ref.shape[0]
     else:
         prob_ref, term_ref = rest
-    rows = query.shape[1]
-    q = query[...].reshape(HB * rows, query.shape[2])
-    score = nt(keys[...], q) * (score_scale * LOG2E) + jnp.concatenate([bias[...]] * HB, axis=1)
+    rows = query.shape[2]
+    q = jnp.concatenate([query[h] for h in range(HB)], axis=1)
+    score = nn(keys[...], q) * (score_scale * LOG2E) + jnp.concatenate([bias[...]] * HB, axis=1)
     peak = jnp.max(score, axis=0, keepdims=True)
     exponent = jnp.exp2(score - peak)
     prob = (exponent * (1.0 / jnp.sum(exponent, axis=0, keepdims=True))).astype(jnp.bfloat16)
@@ -137,25 +138,29 @@
         term = nn(attended[:, h * rows : (h + 1) * rows], scaled)
         part = slice(h * vdim, (h + 1) * vdim)
         if with_sum:
-            term = term + partner[:, part].astype(jnp.float32)
-        term_ref[:, part] = term.astype(jnp.bfloat16)
+            term = (term + partner[:, part].astype(jnp.float32)).astype(jnp.bfloat16)
+            away_ref[:, part] = term[:middle]
+            kept_ref[:, part] = term[middle:]
+        else:
+            term_ref[:, part] = term.astype(jnp.bfloat16)
 
 
 def forward_call(off, heads, query, grad, keys, values_t, bias, weight, partner=None):
-    rows, width = query.shape[1:]
+    width, rows = query.shape[1:]
     vdim = grad.shape[2]
     span = keys.shape[0]
     whole = lambda shape: pl.BlockSpec(shape, lambda i, o: (0, 0))
     by_head = lambda shape: pl.BlockSpec(shape, lambda i, o: (o[0] + i, 0, 0))
     column = lambda height, wide: pl.BlockSpec((height, wide), lambda i, o: (0, i))
     in_specs = [
-        by_head((HB, rows, width)), by_head((HB, rows, vdim)), whole((span, width)),
+        by_head((HB, width, rows)), by_head((HB, rows, vdim)), whole((span, width)),
         whole((LAT, span)), whole((span, rows)), whole((rows, rows)),
     ]
     args = [query, grad, keys, values_t, bias, weight]
     if partner is not None:
         in_specs.append(column(LAT, HB * vdim))
         args.append(partner)
+    terms = 1 if partner is None else 2
     flops = 2 * heads * rows * (span * (width + LAT) + LAT * vdim)
     return pl.pallas_call(
         functools.partial(forward_kernel, partner is not None),
@@ -163,22 +168,21 @@
             num_scalar_prefetch=1,
             grid=(heads // HB,),
             in_specs=in_specs,
-            out_specs=[column(span, HB * rows), column(LAT, HB * vdim)],
+            out_specs=[column(span, HB * rows)] + [column(LAT // terms, HB * vdim)] * terms,
         ),
-        out_shape=[
-            jax.ShapeDtypeStruct((span, heads * rows), jnp.bfloat16),
-            jax.ShapeDtypeStruct((LAT, heads * vdim), jnp.bfloat16),
-        ],
+        out_shape=[jax.ShapeDtypeStruct((span, heads * rows), jnp.bfloat16)]
+        + [jax.ShapeDtypeStruct((LAT // terms, heads * vdim), jnp.bfloat16)] * terms,
         compiler_params=pltpu.CompilerParams(vmem_limit_bytes=48 << 20),
         cost_estimate=pl.CostEstimate(
             flops=flops, bytes_accessed=heads * rows * 4 * (width + span), transcendentals=0),
     )(off, *args)
 
 
-def backward_kernel(off, query, grad, value_weight, prob_ref, keys, weight, out):
-    rows = query.shape[1]
+def backward_kernel(off, query, grad, value_weight, prob_ref, keys, weight, *rest):
+    out = rest[-1]
+    rows = query.shape[2]
     vdim = grad.shape[2]
-    q = query[...].reshape(HB * rows, query.shape[2])
+    q = jnp.concatenate([query[h] for h in range(HB)], axis=1)
     parts = []
     for h in range(HB):
         scaled = (weight[...] * grad[h].astype(jnp.float32)).astype(jnp.bfloat16)
@@ -189,7 +193,7 @@
     prob_grad = nt(keys[:, :LAT], latent_out)
     row_dot = jnp.sum(prob * prob_grad, axis=0, keepdims=True)
     score_grad = (score_scale * prob * (prob_grad - row_dot)).astype(jnp.bfloat16)
-    key_part = nn(score_grad, q)
+    key_part = nt(score_grad, q)
     value_part = nn(prob_b, latent_out)
 
     @pl.when(pl.program_id(0) == 0)
@@ -200,8 +204,8 @@
     out[:, LAT:] += key_part[:, LAT:]
 
 
-def backward_call(off, heads, query, grad, value_weight, prob, keys, weight):
-    rows, width = query.shape[1:]
+def backward_call(off, shift, heads, query, grad, value_weight, prob, keys, weight, after):
+    width, rows = query.shape[1:]
     vdim = grad.shape[2]
     span = keys.shape[0]
     whole = lambda shape: pl.BlockSpec(shape, lambda i, o: (0, 0))
@@ -214,16 +218,17 @@
             num_scalar_prefetch=1,
             grid=(heads // HB,),
             in_specs=[
-                by_head((HB, rows, width)), by_head((HB, rows, vdim)), column(LAT, HB * vdim),
+                by_head((HB, width, rows)), by_head((HB, rows, vdim)),
+                pl.BlockSpec((LAT, HB * vdim), lambda i, o: (0, shift + i)),
                 column(span, HB * rows), whole((span, width)), whole((rows, rows)),
-            ],
+            ] + [pl.BlockSpec(memory_space=pl.ANY)] * len(after),
             out_specs=whole((span, width)),
         ),
         out_shape=jax.ShapeDtypeStruct((span, width), jnp.float32),
         compiler_params=pltpu.CompilerParams(vmem_limit_bytes=48 << 20),
         cost_estimate=pl.CostEstimate(
             flops=flops, bytes_accessed=heads * rows * 4 * (width + span), transcendentals=0),
-    )(off, query, grad, value_weight, prob, keys, weight)
+    )(off, query, grad, value_weight, prob, keys, weight, *after)
 
 
 def key_kernel(n, first, second, out, term, got, send, recv):
@@ -267,13 +272,20 @@
     )(first, second)
 
 
-def finish_kernel(m, count, *refs):
-    parts, (out, across, mine, other, x_send, x_recv, c_send, c_recv) = refs[:count], refs[count:]
+def finish_kernel(m, count, terms, *refs):
+    out, across, part, mine, other, x_send, x_recv, c_send, c_recv = refs[count * terms + 1 :]
+    parts = []
+    for j in range(count):
+        total = refs[j * terms][...].astype(jnp.float32)
+        for k in range(1, terms):
+            total = total + refs[j * terms + k][...].astype(jnp.float32)
+        part[j] = total.astype(jnp.bfloat16)
+        parts.append(part.at[j])
     me = lax.axis_index("dp")
     core = lax.rem(me, 2)
     chip = me // 2
     chips = m // 2
-    wide = parts[0].shape[1]
+    wide = part.shape[2]
     half = wide * count
     partner = {"dp": chip * 2 + (1 - core)}
     peers = [{"dp": lax.rem(chip + d, chips) * 2 + core} for d in range(1, chips)]
@@ -309,18 +321,20 @@
             other[j].astype(jnp.float32))
 
 
-def finish_call(m, parts):
+def finish_call(m, parts, after):
     count = len(parts)
-    rows, wide = parts[0].shape
+    terms = len(parts[0])
+    rows, wide = parts[0][0].shape
     vm = pl.BlockSpec(memory_space=VMEM)
     chips = m // 2
     return pl.pallas_call(
-        functools.partial(finish_kernel, m, count),
+        functools.partial(finish_kernel, m, count, terms),
         out_shape=jax.ShapeDtypeStruct((rows, 2 * wide * count), jnp.float32),
-        in_specs=[vm] * count,
+        in_specs=[vm] * (count * terms) + [pl.BlockSpec(memory_space=pl.ANY)],
         out_specs=vm,
         scratch_shapes=[
             VMEM((count, chips, rows, wide), jnp.bfloat16),
+            VMEM((count, rows, wide), jnp.bfloat16),
             VMEM((count, rows, wide), jnp.bfloat16),
             VMEM((count, rows, wide), jnp.bfloat16),
             pltpu.SemaphoreType.DMA((count, chips - 1)),
@@ -331,10 +345,54 @@
         compiler_params=pltpu.CompilerParams(
             collective_id=2, has_side_effects=True, vmem_limit_bytes=24 << 20),
         cost_estimate=pl.CostEstimate(flops=1 << 20, bytes_accessed=6 << 20, transcendentals=0),
-    )(*parts)
+    )(*[term for row in parts for term in row], after)
 
 
 CHUNKS = 2
+LINE = 4
+PAIR = 2
+
+
+def gate_kernel(held, *rest):
+    pass
+
+
+def held_until(held, *after):
+    anywhere = pl.BlockSpec(memory_space=pl.ANY)
+    return pl.pallas_call(
+        gate_kernel,
+        out_shape=jax.ShapeDtypeStruct(held.shape, held.dtype),
+        in_specs=[anywhere] * (1 + len(after)),
+        out_specs=anywhere,
+        input_output_aliases={0: 0},
+    )(held, *after)
+
+
+def pair_terms(away, kept, n):
+    came = lax.ppermute(away, "ctx", [(i, i ^ 1) for i in range(n)])
+    return (kept.astype(jnp.float32) + came.astype(jnp.float32)).astype(jnp.bfloat16)
+
+
+def line_terms(pair, n):
+    rows = pair.shape[0] // LINE
+    came = [pair[:rows]]
+    for d in range(1, LINE):
+        path = [(i, (i // PAIR + d) % LINE * PAIR + i % PAIR) for i in range(n)]
+        came.append(lax.ppermute(pair[d * rows : (d + 1) * rows], "ctx", path))
+    return came
+
+
+def in_route_order(values_t, n):
+    if n != LINE * PAIR:
+        return values_t
+    me = lax.axis_index("ctx")
+    width, span = values_t.shape
+    blocks = values_t.reshape(LINE, PAIR, width // n, span)
+    blocks = lax.dynamic_slice_in_dim(
+        jnp.concatenate([blocks, blocks], axis=0), me // PAIR, LINE, 0)
+    away = lax.dynamic_slice_in_dim(blocks, 1 - me % PAIR, 1, 1)
+    kept = lax.dynamic_slice_in_dim(blocks, me % PAIR, 1, 1)
+    return jnp.concatenate([away, kept], axis=1).transpose(1, 0, 2, 3).reshape(width, span)
 
 
 def per_device(latent, query, out_grad, value_weight, doc_lengths, resumed, groups, reward):
@@ -346,11 +404,12 @@
     quarter = half // CHUNKS
     vdim = out_grad.shape[3]
     swap = [(i, i ^ 1) for i in range(m)]
+    keys, bias, weight = start_call(n, doc_lengths, resumed, latent[0], groups, reward)
     half_rows = lax.dynamic_slice_in_dim(value_weight, core * half * vdim, half * vdim, 1)
+    half_rows, weight = lax.optimization_barrier((half_rows, weight))
     own_weight = lax.all_gather(half_rows, "ctx", axis=0, tiled=True)
-    keys, bias, weight = start_call(n, doc_lengths, resumed, latent[0], groups, reward)
-    values_t = keys[:, :LAT].T
-    q = jnp.transpose(query[0], (1, 0, 2))
+    values_t = in_route_order(keys[:, :LAT].T, n)
+    q = jnp.transpose(query[0], (1, 2, 0))
     grad = jnp.transpose(out_grad[0], (1, 0, 2))
     own_at = [((core * half + j * quarter) // HB).astype(jnp.int32).reshape(1) for j in range(CHUNKS)]
     other_at = [(((1 - core) * half + j * quarter) // HB).astype(jnp.int32).reshape(1)
@@ -360,22 +419,31 @@
         prob, term = forward_call(other_at[j], quarter, q, grad, keys, values_t, bias, weight)
         other_prob.append(prob)
         arrived.append(lax.ppermute(term, "dp", swap))
+    routed = n == LINE * PAIR
     for j in range(CHUNKS):
-        prob, term = forward_call(
+        prob, away, kept = forward_call(
             own_at[j], quarter, q, grad, keys, values_t, bias, weight, arrived[j])
         own_prob.append(prob)
-        sums.append(lax.psum_scatter(term, "ctx", scatter_dimension=0, tiled=True))
+        if routed:
+            sums.append(pair_terms(away, kept, n))
+        else:
+            sums.append([lax.psum_scatter(
+                jnp.concatenate([away, kept], axis=0), "ctx", scatter_dimension=0, tiled=True)])
+    own_weight = held_until(own_weight, own_prob[-1])
     other_weight = lax.ppermute(own_weight, "dp", swap)
     pieces = []
     for at, weights, probs in ((own_at, own_weight, own_prob), (other_at, other_weight, other_prob)):
         for j in range(CHUNKS):
+            after = pieces[-1:]
+            if routed and weights is own_weight:
+                after = after + [sums[j]]
+                sums[j] = line_terms(sums[j], n)
             pieces.append(backward_call(
-                at[j], quarter, q, grad, weights[:, j * quarter * vdim : (j + 1) * quarter * vdim],
-                probs[j], keys, weight))
+                at[j], j * quarter // HB, quarter, q, grad, weights, probs[j], keys, weight, after))
     first = sum(pieces[1 : len(pieces) // 2], pieces[0])
     second = sum(pieces[len(pieces) // 2 + 1 :], pieces[len(pieces) // 2])
     latent_grad = key_call(n, first, second)
-    weight_grad = finish_call(m, sums)
+    weight_grad = finish_call(m, sums, latent_grad)
     return (latent_grad[None], weight_grad)
 
 

time: 324 us -> 237 us (0.73)
  waiting for transfers between devices: 138 us -> 75.7 us
  local copies, waits for them, and re-layouts: 46.3 us -> 17 us
  starting transfers between devices: 4.93 us -> 13.7 us
  Pallas kernels: 120 us -> 113 us
    reduce_scatter x2 -> x0, waiting for transfers between devices: 129 us -> none  [per_device(): sums.append(lax.psum_scatter(term, 'ctx', scatter_dimension=0, tiled=True))]
    all_gather x1, waiting for transfers between devices: 0.02 us -> 41.5 us  [per_device(): own_weight = lax.all_gather(half_rows, 'ctx', axis=0, tiled=True)]
    ppermute x0 -> x8, waiting for transfers between devices: none -> 34.1 us  [the longest x2 34.1 us: pair_terms(): came = lax.ppermute(away, 'ctx', [(i, i ^ 1) for i in range(n)])]
    unnamed x35 -> x30, local copies, waits for them, and re-layouts: 35.3 us -> 15.7 us
    slice x2, local copies, waits for them, and re-layouts: 9.86 us -> 0.2 us  [line_terms(): came.append(lax.ppermute(pair[d * rows:(d + 1) * rows], 'ctx', path))]
    ppermute x0 -> x8, starting transfers between devices: none -> 8.99 us  [the longest x6 7.45 us: line_terms(): came.append(lax.ppermute(pair[d * rows:(d + 1) * rows], 'ctx', path))]
    ppermute x2, waiting for transfers between devices: 8.26 us -> 0.01 us  [per_device(): arrived.append(lax.ppermute(term, 'dp', swap))]
    pallas_call x1, Pallas kernels: 20.9 us -> 14.5 us  [start_call(): pl.pallas_call(functools.partial(start_kernel, n, lengths.shape[1]), out_...]
  transfers between devices with their start and end apart: 6 -> 12, of which waited for: 4 -> 3; matrix products, arithmetic and copies ran while one was open for 8% -> 3% of each run, Pallas kernels for 26% -> 34%
where the time goes in v1:
time: 237 us; the launch traced here: 236 us
  Pallas kernels  113 us (48%)
  waiting for transfers between devices  75.7 us (32%)
  local copies, waits for them, and re-layouts  17 us (7%)
  between operations  14.4 us (6%)
  starting transfers between devices  13.7 us (6%)
  other arithmetic  2.52 us (1%)
    all_gather x1, waiting for transfers between devices, per_device(): own_weight = lax.all_gather(half_rows, 'ctx', axis=0, tiled=True)  41.5 us
    ppermute x2, waiting for transfers between devices, pair_terms(): came = lax.ppermute(away, 'ctx', [(i, i ^ 1) for i in range(n)])  34.1 us
    pallas_call x4, Pallas kernels, backward_call(): pl.pallas_call(backward_kernel, grid_spec=pltpu.PrefetchScalarGridSpec(nu...  33.7 us
    pallas_call x4, Pallas kernels, forward_call(): pl.pallas_call(functools.partial(forward_kernel, partner is not None), gr...  29.9 us
    pallas_call x1, Pallas kernels, finish_call(): pl.pallas_call(functools.partial(finish_kernel, m, count, terms), out_sha...  18.1 us
    pallas_call x1, Pallas kernels, key_call(): pl.pallas_call(functools.partial(key_kernel, n), out_shape=jax.ShapeDtype...  16.6 us
    unnamed x30, local copies, waits for them, and re-layouts  15.7 us
    pallas_call x1, Pallas kernels, start_call(): pl.pallas_call(functools.partial(start_kernel, n, lengths.shape[1]), out_...  14.5 us
  transfers between devices with their start and end apart: 12, of which 3 were waited for; matrix products, arithmetic and copies ran while one was open for 3% of the time, Pallas kernels for 34%

profile of v1, /device:TPU:5, one launch (start us, length us, event | category | flops | bytes accessed | tf_op | source)
XLA Modules:
  0.0 236.1 jit_solution(7361698278053058696)
XLA Ops:
  7.2 0.0 copy-start
  7.2 0.0 all-gather.2.cloned.1.call-start
  7.2 1.1 copy.17
  8.4 0.1 copy-done
  8.5 0.8 constant_dynamic-slice_fusion
  9.3 0.7 copy-done.8
  10.0 0.7 copy-done.9
  10.6 0.7 copy-done.10
  11.3 0.7 copy-done.11
  11.9 14.5 %shard_map.95 = (bf16[512,576]{1,0:T(8,128)(2,1)S(1)}, f32[512,128]{1,0:T(8,128)S(1)}, f32[128,128]{1,0:T(8,128)S(1)}) custom-call(s32[1,8]{1,0:T(1,128)S(1)} %copy-done.8, s32[1,8]{1,0:T(1,128)S(1)} %copy-done.9, bf16[128,576]{1,0:T(8,128)(2,1)S(1)} %bitcast.33, s32[1,128]{1,0:T(1,128)S(1)} %copy-done.10, f32[1,128]{1,0:T(1,128)S(1)} %copy-done.11), custom_call_target="tpu_custom_call" | custom-call | flops 1048576 | bytes 2097152 | tf_op jit(solution)/shard_map/pallas_call | solution.py:90
  26.5 0.0 all-gather.2.cloned.1.call-update
  26.6 0.2 copy.18
  26.8 0.2 fusion.1
  27.0 0.1 maximum_bitcast_fusion
  27.1 4.3 %copy.22 = bf16[1,128,64,128]{3,1,2,0:T(8,128)(2,1)} copy(bf16[1,128,64,128]{3,2,1,0:T(8,128)(2,1)} %param.10) | data formatting | bytes 4194304 | tf_op args[2]
  31.4 7.7 %shard_map.96 = (bf16[512,2048]{1,0:T(8,128)(2,1)S(1)}, bf16[512,2048]{1,0:T(8,128)(2,1)}) custom-call(s32[1]{0:T(128)} %bitcast.13.off, bf16[64,576,128]{2,1,0:T(8,128)(2,1)} %bitcast.34, bf16[64,128,128]{2,1,0:T(8,128)(2,1)} %bitcast.20, bf16[512,576]{1,0:T(8,128)(2,1)S(1)} %get-tuple-element.19.keys, bf16[512,512]{1,0:T(8,128)(2,1)S(1)} %bitcast.28, ...), custom_call_target="tpu_custom_call" | custom-call | flops 2550136832 | bytes 8912896 | tf_op jit(solution)/shard_map/pallas_call | solution.py:165
  39.1 1.4 copy-done.5
  40.5 2.8 %collective-permute-start = (bf16[512,2048]{1,0:T(8,128)(2,1)}, bf16[512,2048]{1,0:T(8,128)(2,1)}, u32[]{:S(2)}, u32[]{:S(2)}) collective-permute-start(bf16[512,2048]{1,0:T(8,128)(2,1)} %get-tuple-element.22), channel_id=1, source_target_pairs={{0,8},{8,0},{16,24},{24,16},{1,9},{9,1},{17,25},{25,17},{2,10},{10... | collective-permute-start | bytes 6291464 | tf_op jit(solution)/shard_map/ppermute | solution.py:421
  43.3 7.7 %shard_map.99 = (bf16[512,2048]{1,0:T(8,128)(2,1)S(1)}, bf16[512,2048]{1,0:T(8,128)(2,1)}) custom-call(s32[1]{0:T(128)} %bitcast.14.off, bf16[64,576,128]{2,1,0:T(8,128)(2,1)} %bitcast.35, bf16[64,128,128]{2,1,0:T(8,128)(2,1)} %bitcast.21, bf16[512,576]{1,0:T(8,128)(2,1)S(1)} %get-tuple-element.19.keys, bf16[512,512]{1,0:T(8,128)(2,1)S(1)} %bitcast.29, ...), custom_call_target="tpu_custom_call" | custom-call | flops 2550136832 | bytes 8912896 | tf_op jit(solution)/shard_map/pallas_call | solution.py:165
  51.0 1.4 copy-done.6
  52.3 0.0 collective-permute-start.1
  52.3 0.0 collective-permute-done.rest_0_
  52.3 7.3 %shard_map.97 = (bf16[512,2048]{1,0:T(8,128)(2,1)S(1)}, bf16[256,2048]{1,0:T(8,128)(2,1)S(1)}, bf16[256,2048]{1,0:T(8,128)(2,1)S(1)}) custom-call(s32[1]{0:T(128)} %bitcast.6.off, bf16[64,576,128]{2,1,0:T(8,128)(2,1)} %bitcast.36, bf16[64,128,128]{2,1,0:T(8,128)(2,1)} %bitcast.22, bf16[512,576]{1,0:T(8,128)(2,1)S(1)} %get-tuple-element.19.keys, ...), custom_call_target="tpu_custom_call" | custom-call | flops 2550136832 | bytes 8912896 | tf_op jit(solution)/shard_map/pallas_call | solution.py:165
  59.6 1.3 copy-done.4
  60.9 1.0 copy-done.12
  61.9 41.5 %all-gather.2.cloned.1.call-done.held = bf16[512,4096]{1,0:T(8,128)(2,1)} async-done(((bf16[64,4096]{1,0:T(8,128)(2,1)}), bf16[512,4096]{1,0:T(8,128)(2,1)}) %all-gather.2.cloned.1.call-update) | async-done | bytes 4194320 | tf_op jit(solution)/shard_map/all_gather | solution.py:410
  103.5 1.9 collective-permute-start.4
  105.3 1.2 collective-permute-start.3
  106.5 0.0 collective-permute-done.1.rest_0_
  106.5 7.2 %shard_map.100 = (bf16[512,2048]{1,0:T(8,128)(2,1)S(1)}, bf16[256,2048]{1,0:T(8,128)(2,1)S(1)}, bf16[256,2048]{1,0:T(8,128)(2,1)S(1)}) custom-call(s32[1]{0:T(128)} %bitcast.off, bf16[64,576,128]{2,1,0:T(8,128)(2,1)} %bitcast.37, bf16[64,128,128]{2,1,0:T(8,128)(2,1)} %bitcast.23, bf16[512,576]{1,0:T(8,128)(2,1)S(1)} %get-tuple-element.19.keys, ...), custom_call_target="tpu_custom_call" | custom-call | flops 2550136832 | bytes 8912896 | tf_op jit(solution)/shard_map/pallas_call | solution.py:165
  113.8 0.3 collective-permute-start.2
  114.1 16.3 %collective-permute-done.3 = bf16[256,2048]{1,0:T(8,128)(2,1)} collective-permute-done((bf16[256,2048]{1,0:T(8,128)(2,1)}, bf16[256,2048]{1,0:T(8,128)(2,1)}, u32[]{:S(2)}, u32[]{:S(2)}) %collective-permute-start.3) | collective-permute-done | bytes 1048608 | tf_op jit(solution)/shard_map/ppermute | solution.py:372
  130.4 1.6 add_convert_fusion.rest_1_
  132.0 0.1 fusion.2
  132.2 1.4 collective-permute-start.10
  133.5 0.2 collective-permute-start.8
  133.7 1.3 collective-permute-start.9
  135.0 17.8 %collective-permute-done.2 = bf16[256,2048]{1,0:T(8,128)(2,1)S(1)} collective-permute-done((bf16[256,2048]{1,0:T(8,128)(2,1)S(1)}, bf16[256,2048]{1,0:T(8,128)(2,1)S(1)}, u32[]{:S(2)}, u32[]{:S(2)}) %collective-permute-start.2) | collective-permute-done | bytes 1048608 | tf_op jit(solution)/shard_map/ppermute | solution.py:372
  152.8 0.4 add_convert_fusion.1.rest_0_
  153.2 0.1 fusion.3
  153.3 0.8 collective-permute-start.5
  154.1 0.3 copy-done.2
  154.4 8.4 %shard_map.101.rest_0_ = f32[512,576]{1,0:T(8,128)S(1)} custom-call(s32[1]{0:T(128)} %bitcast.off, bf16[64,576,128]{2,1,0:T(8,128)(2,1)} %bitcast.38, bf16[64,128,128]{2,1,0:T(8,128)(2,1)S(1)} %bitcast.25, bf16[512,4096]{1,0:T(8,128)(2,1)} %shard_map.98.value_weight, bf16[512,2048]{1,0:T(8,128)(2,1)} %copy-done.7, ...), custom_call_target="tpu_custom_call" | custom-call | flops 3623878656 | bytes 8912896 | tf_op jit(solution)/shard_map/pallas_call | solution.py:215
  162.8 8.5 %shard_map.102.rest_0_ = f32[512,576]{1,0:T(8,128)S(1)} custom-call(s32[1]{0:T(128)} %bitcast.6.off, bf16[64,576,128]{2,1,0:T(8,128)(2,1)} %bitcast.39, bf16[64,128,128]{2,1,0:T(8,128)(2,1)} %bitcast.24, bf16[512,4096]{1,0:T(8,128)(2,1)} %shard_map.98.value_weight, bf16[512,2048]{1,0:T(8,128)(2,1)} %copy-done.4, ...), custom_call_target="tpu_custom_call" | custom-call | flops 3623878656 | bytes 8912896 | tf_op jit(solution)/shard_map/pallas_call | solution.py:215
  171.3 0.0 copy-start.3
  171.3 0.1 add.58.first
  171.5 0.0 collective-permute-done.4.value_weight
  171.5 1.4 collective-permute-start.6
  172.9 0.1 copy-done.3
  172.9 8.4 %shard_map.103.rest_0_ = f32[512,576]{1,0:T(8,128)S(1)} custom-call(s32[1]{0:T(128)} %bitcast.14.off, bf16[64,576,128]{2,1,0:T(8,128)(2,1)} %bitcast.40, bf16[64,128,128]{2,1,0:T(8,128)(2,1)S(1)} %bitcast.26, bf16[512,4096]{1,0:T(8,128)(2,1)} %collective-permute-done.4.value_weight, bf16[512,2048]{1,0:T(8,128)(2,1)} %copy-done.6, ...), custom_call_target="tpu_custom_call" | custom-call | flops 3623878656 | bytes 8912896 | tf_op jit(solution)/shard_map/pallas_call | solution.py:215
  181.3 0.0 collective-permute-done.10.refs_7_
  181.3 2.5 %collective-permute-start.7 = (bf16[64,2048]{1,0:T(8,128)(2,1)S(1)}, bf16[64,2048]{1,0:T(8,128)(2,1)S(1)}, u32[]{:S(2)}, u32[]{:S(2)}) collective-permute-start(bf16[64,2048]{1,0:T(8,128)(2,1)S(1)} %get-tuple-element.40), channel_id=1, source_target_pairs={{0,6},{1,7},{2,0},{3,1},{4,2},{5,3},{6,4},{7,5},{8,14},{9,15},{10,... | collective-permute-start | bytes 786440 | tf_op jit(solution)/shard_map/ppermute | solution.py:381
  183.8 8.4 %shard_map.104 = f32[512,576]{1,0:T(8,128)S(1)} custom-call(s32[1]{0:T(128)} %bitcast.13.off, bf16[64,576,128]{2,1,0:T(8,128)(2,1)} %bitcast.41, bf16[64,128,128]{2,1,0:T(8,128)(2,1)S(1)} %bitcast.27, bf16[512,4096]{1,0:T(8,128)(2,1)} %collective-permute-done.4.value_weight, bf16[512,2048]{1,0:T(8,128)(2,1)} %copy-done.5, ...), custom_call_target="tpu_custom_call" | custom-call | flops 3623878656 | bytes 8912896 | tf_op jit(solution)/shard_map/pallas_call | solution.py:215
  192.2 0.1 add.59.second
  192.3 16.6 %shard_map.105.refs_8_ = f32[128,576]{1,0:T(8,128)S(1)} custom-call(f32[512,576]{1,0:T(8,128)S(1)} %add.58.first, f32[512,576]{1,0:T(8,128)S(1)} %add.59.second), custom_call_target="tpu_custom_call" | custom-call | flops 1048576 | bytes 3145728 | tf_op jit(solution)/shard_map/pallas_call | solution.py:258
  208.9 0.0 collective-permute-done.8.refs_5_
  208.9 0.0 collective-permute-done.9.refs_6_
  209.0 0.0 collective-permute-done.5.refs_1_
  209.0 0.0 collective-permute-done.6.refs_2_
  209.0 0.0 collective-permute-done.7.refs_3_
  209.0 18.1 %shard_map.106 = f32[64,8192]{1,0:T(8,128)S(1)} custom-call(bf16[64,2048]{1,0:T(8,128)(2,1)S(1)} %get-tuple-element.43.refs_0_, bf16[64,2048]{1,0:T(8,128)(2,1)S(1)} %collective-permute-done.5.refs_1_, bf16[64,2048]{1,0:T(8,128)(2,1)S(1)} %collective-permute-done.6.refs_2_, bf16[64,2048]{1,0:T(8,128)(2,1)S(1)} %collective-permute-done.7.refs_3_, ...), custom_call_target="tpu_custom_call" | custom-call | flops 1048576 | bytes 6291456 | tf_op jit(solution)/shard_map/pallas_call | solution.py:330
  227.1 0.0 copy-start.1
  227.1 0.9 copy.20
  228.0 1.3 copy.25
  (15 shorter events, 0.1 us)
Async XLA Ops:
  7.2 1.3 copy-start
  7.2 96.3 %all-gather.2.cloned.1.call-start = ((), (), s32[]{:S(2)}) async-start(), calls=%async_computation | async-start | bytes 4718592 | tf_op jit(solution)/shard_map/all_gather | solution.py:410
  9.3 0.7 copy-start.8
  10.0 0.7 copy-start.9
  10.6 0.7 copy-start.10
  11.3 0.7 copy-start.11
  39.1 1.4 copy-start.5
  40.5 11.9 %collective-permute-start = (bf16[512,2048]{1,0:T(8,128)(2,1)}, bf16[512,2048]{1,0:T(8,128)(2,1)}, u32[]{:S(2)}, u32[]{:S(2)}) collective-permute-start(bf16[512,2048]{1,0:T(8,128)(2,1)} %get-tuple-element.22), channel_id=1, source_target_pairs={{0,8},{8,0},{16,24},{24,16},{1,9},{9,1},{17,25},{25,17},{2,10},{10... | collective-permute-start | bytes 6291464 | tf_op jit(solution)/shard_map/ppermute | solution.py:421
  51.0 1.4 copy-start.6
  52.3 54.2 %collective-permute-start.1 = (bf16[512,2048]{1,0:T(8,128)(2,1)}, bf16[512,2048]{1,0:T(8,128)(2,1)}, u32[]{:S(2)}, u32[]{:S(2)}) collective-permute-start(bf16[512,2048]{1,0:T(8,128)(2,1)} %get-tuple-element.24), channel_id=1, source_target_pairs={{0,8},{8,0},{16,24},{24,16},{1,9},{9,1},{17,25},{25,17},{2,10},{10... | collective-permute-start | bytes 6291464 | tf_op jit(solution)/shard_map/ppermute | solution.py:421
  59.6 1.3 copy-start.4
  60.9 1.0 copy-start.12
  103.5 68.0 %collective-permute-start.4 = (bf16[512,4096]{1,0:T(8,128)(2,1)}, bf16[512,4096]{1,0:T(8,128)(2,1)}, u32[]{:S(2)}, u32[]{:S(2)}) collective-permute-start(bf16[512,4096]{1,0:T(8,128)(2,1)} %shard_map.98.value_weight), channel_id=1, source_target_pairs={{0,8},{8,0},{16,24},{24,16},{1,9},{9,1},{17,25},{25,17},{2,10},{10... | collective-permute-start | bytes 12582920 | tf_op jit(solution)/shard_map/ppermute | solution.py:433
  105.3 25.1 %collective-permute-start.3 = (bf16[256,2048]{1,0:T(8,128)(2,1)}, bf16[256,2048]{1,0:T(8,128)(2,1)}, u32[]{:S(2)}, u32[]{:S(2)}) collective-permute-start(bf16[256,2048]{1,0:T(8,128)(2,1)} %copy-done.12), channel_id=1, source_target_pairs={{0,1},{1,0},{2,3},{3,2},{4,5},{5,4},{6,7},{7,6},{8,9},{9,8},{10,11... | collective-permute-start | bytes 3145736 | tf_op jit(solution)/shard_map/ppermute | solution.py:372
  113.8 18.4 %copy-start.7 = (bf16[512,2048]{1,0:T(8,128)(2,1)}, bf16[512,2048]{1,0:T(8,128)(2,1)S(1)}, u32[]{:S(2)}) copy-start(bf16[512,2048]{1,0:T(8,128)(2,1)S(1)} %get-tuple-element.25.prob_ref) | copy-start | bytes 6291460
  113.8 39.0 %collective-permute-start.2 = (bf16[256,2048]{1,0:T(8,128)(2,1)S(1)}, bf16[256,2048]{1,0:T(8,128)(2,1)S(1)}, u32[]{:S(2)}, u32[]{:S(2)}) collective-permute-start(bf16[256,2048]{1,0:T(8,128)(2,1)S(1)} %get-tuple-element.27), channel_id=1, source_target_pairs={{0,1},{1,0},{2,3},{3,2},{4,5},{5,4},{6,7},{7,6},{8,9},{9,8},{10,11... | collective-permute-start | bytes 3145736 | tf_op jit(solution)/shard_map/ppermute | solution.py:372
  132.2 49.1 %collective-permute-start.10 = (bf16[64,2048]{1,0:T(8,128)(2,1)S(1)}, bf16[64,2048]{1,0:T(8,128)(2,1)S(1)}, u32[]{:S(2)}, u32[]{:S(2)}) collective-permute-start(bf16[64,2048]{1,0:T(8,128)(2,1)S(1)} %get-tuple-element.36), channel_id=1, source_target_pairs={{0,6},{1,7},{2,0},{3,1},{4,2},{5,3},{6,4},{7,5},{8,14},{9,15},{10,... | collective-permute-start | bytes 786440 | tf_op jit(solution)/shard_map/ppermute | solution.py:381
  133.5 75.4 %collective-permute-start.8 = (bf16[64,2048]{1,0:T(8,128)(2,1)S(1)}, bf16[64,2048]{1,0:T(8,128)(2,1)S(1)}, u32[]{:S(2)}, u32[]{:S(2)}) collective-permute-start(bf16[64,2048]{1,0:T(8,128)(2,1)S(1)} %get-tuple-element.38), channel_id=1, source_target_pairs={{0,2},{1,3},{2,4},{3,5},{4,6},{5,7},{6,0},{7,1},{8,10},{9,11},{10,... | collective-permute-start | bytes 786440 | tf_op jit(solution)/shard_map/ppermute | solution.py:381
  133.7 75.3 %collective-permute-start.9 = (bf16[64,2048]{1,0:T(8,128)(2,1)S(1)}, bf16[64,2048]{1,0:T(8,128)(2,1)S(1)}, u32[]{:S(2)}, u32[]{:S(2)}) collective-permute-start(bf16[64,2048]{1,0:T(8,128)(2,1)S(1)} %get-tuple-element.37), channel_id=1, source_target_pairs={{0,4},{1,5},{2,6},{3,7},{4,0},{5,1},{6,2},{7,3},{8,12},{9,13},{10,... | collective-permute-start | bytes 786440 | tf_op jit(solution)/shard_map/ppermute | solution.py:381
  152.8 1.6 copy-start.2
  153.3 55.7 %collective-permute-start.5 = (bf16[64,2048]{1,0:T(8,128)(2,1)S(1)}, bf16[64,2048]{1,0:T(8,128)(2,1)S(1)}, u32[]{:S(2)}, u32[]{:S(2)}) collective-permute-start(bf16[64,2048]{1,0:T(8,128)(2,1)S(1)} %get-tuple-element.42), channel_id=1, source_target_pairs={{0,2},{1,3},{2,4},{3,5},{4,6},{5,7},{6,0},{7,1},{8,10},{9,11},{10,... | collective-permute-start | bytes 786440 | tf_op jit(solution)/shard_map/ppermute | solution.py:381
  171.3 1.6 copy-start.3
  171.5 37.5 %collective-permute-start.6 = (bf16[64,2048]{1,0:T(8,128)(2,1)S(1)}, bf16[64,2048]{1,0:T(8,128)(2,1)S(1)}, u32[]{:S(2)}, u32[]{:S(2)}) collective-permute-start(bf16[64,2048]{1,0:T(8,128)(2,1)S(1)} %get-tuple-element.41), channel_id=1, source_target_pairs={{0,4},{1,5},{2,6},{3,7},{4,0},{5,1},{6,2},{7,3},{8,12},{9,13},{10,... | collective-permute-start | bytes 786440 | tf_op jit(solution)/shard_map/ppermute | solution.py:381
  181.3 27.7 %collective-permute-start.7 = (bf16[64,2048]{1,0:T(8,128)(2,1)S(1)}, bf16[64,2048]{1,0:T(8,128)(2,1)S(1)}, u32[]{:S(2)}, u32[]{:S(2)}) collective-permute-start(bf16[64,2048]{1,0:T(8,128)(2,1)S(1)} %get-tuple-element.40), channel_id=1, source_target_pairs={{0,6},{1,7},{2,0},{3,1},{4,2},{5,3},{6,4},{7,5},{8,14},{9,15},{10,... | collective-permute-start | bytes 786440 | tf_op jit(solution)/shard_map/ppermute | solution.py:381
  227.1 2.2 copy-start.1
Sparse Core Ops, SparseCore 0:
  26.6 76.7 all-gather.1

commit v2 on v1

--- a/solution.py
+++ b/solution.py
@@ -51,7 +51,7 @@
             src_ref=latent, dst_ref=keys.at[pl.ds((BACK - d) * rows, rows)],
             send_sem=key_send.at[d - 1], recv_sem=key_recv.at[d - 1],
             device_id=target, device_id_type=MESH))
-        moves[-1].start()
+        pl.when(me + d < n)(moves[-1].start)
     keys[BACK * rows :, :] = latent[...]
     first = me * rows
     query_pos = first + lax.broadcasted_iota(jnp.int32, (1, rows), 1)
@@ -78,8 +78,13 @@
         mean = jnp.where(ids == g, sums[g : g + 1] / sums[NGROUP + g : NGROUP + g + 1], mean)
     token = 0.125 * (gains - mean)
     weight[...] = jnp.transpose(jnp.broadcast_to(token, (rows, rows)))
-    for copy in moves:
-        copy.wait()
+    for d in range(1, BACK + 1):
+        pl.when(me + d < n)(moves[d - 1].wait_send)
+        pl.when(me >= d)(moves[d - 1].wait_recv)
+
+        @pl.when(me < d)
+        def _(d=d):
+            keys[(BACK - d) * rows : (BACK + 1 - d) * rows, :] = jnp.zeros_like(latent)
 
 
 def start_call(n, lengths, resumed, latent, groups, reward):
@@ -120,8 +125,7 @@
 
 def forward_kernel(with_sum, off, query, grad, keys, values_t, bias, weight, *rest):
     if with_sum:
-        partner, prob_ref, away_ref, kept_ref = rest
-        middle = away_ref.shape[0]
+        partner, prob_ref, term_ref = rest
     else:
         prob_ref, term_ref = rest
     rows = query.shape[2]
@@ -138,11 +142,8 @@
         term = nn(attended[:, h * rows : (h + 1) * rows], scaled)
         part = slice(h * vdim, (h + 1) * vdim)
         if with_sum:
-            term = (term + partner[:, part].astype(jnp.float32)).astype(jnp.bfloat16)
-            away_ref[:, part] = term[:middle]
-            kept_ref[:, part] = term[middle:]
-        else:
-            term_ref[:, part] = term.astype(jnp.bfloat16)
+            term = term + partner[:, part].astype(jnp.float32)
+        term_ref[:, part] = term.astype(jnp.bfloat16)
 
 
 def forward_call(off, heads, query, grad, keys, values_t, bias, weight, partner=None):
@@ -160,7 +161,6 @@
     if partner is not None:
         in_specs.append(column(LAT, HB * vdim))
         args.append(partner)
-    terms = 1 if partner is None else 2
     flops = 2 * heads * rows * (span * (width + LAT) + LAT * vdim)
     return pl.pallas_call(
         functools.partial(forward_kernel, partner is not None),
@@ -168,10 +168,12 @@
             num_scalar_prefetch=1,
             grid=(heads // HB,),
             in_specs=in_specs,
-            out_specs=[column(span, HB * rows)] + [column(LAT // terms, HB * vdim)] * terms,
+            out_specs=[column(span, HB * rows), column(LAT, HB * vdim)],
         ),
-        out_shape=[jax.ShapeDtypeStruct((span, heads * rows), jnp.bfloat16)]
-        + [jax.ShapeDtypeStruct((LAT // terms, heads * vdim), jnp.bfloat16)] * terms,
+        out_shape=[
+            jax.ShapeDtypeStruct((span, heads * rows), jnp.bfloat16),
+            jax.ShapeDtypeStruct((LAT, heads * vdim), jnp.bfloat16),
+        ],
         compiler_params=pltpu.CompilerParams(vmem_limit_bytes=48 << 20),
         cost_estimate=pl.CostEstimate(
             flops=flops, bytes_accessed=heads * rows * 4 * (width + span), transcendentals=0),
@@ -204,7 +206,7 @@
     out[:, LAT:] += key_part[:, LAT:]
 
 
-def backward_call(off, shift, heads, query, grad, value_weight, prob, keys, weight, after):
+def backward_call(off, heads, query, grad, value_weight, prob, keys, weight, after):
     width, rows = query.shape[1:]
     vdim = grad.shape[2]
     span = keys.shape[0]
@@ -219,7 +221,7 @@
             grid=(heads // HB,),
             in_specs=[
                 by_head((HB, width, rows)), by_head((HB, rows, vdim)),
-                pl.BlockSpec((LAT, HB * vdim), lambda i, o: (0, shift + i)),
+                pl.BlockSpec((LAT, HB * vdim), lambda i, o: (0, o[1] + i)),
                 column(span, HB * rows), whole((span, width)), whole((rows, rows)),
             ] + [pl.BlockSpec(memory_space=pl.ANY)] * len(after),
             out_specs=whole((span, width)),
@@ -243,12 +245,15 @@
             src_ref=term.at[pl.ds((BACK - d) * rows, rows)], dst_ref=got.at[d - 1],
             send_sem=send.at[d - 1], recv_sem=recv.at[d - 1],
             device_id={"ctx": lax.rem(me + n - d, n)}, device_id_type=MESH))
-        moves[-1].start()
-    total = term[BACK * rows :, :].astype(jnp.float32)
+        pl.when(me >= d)(moves[-1].start)
+    out[...] = term[BACK * rows :, :].astype(jnp.float32)
     for d in range(1, BACK + 1):
-        moves[d - 1].wait()
-        total = total + jnp.where(me + d < n, got[d - 1].astype(jnp.float32), 0.0)
-    out[...] = total
+        pl.when(me >= d)(moves[d - 1].wait_send)
+
+        @pl.when(me + d < n)
+        def _(d=d):
+            moves[d - 1].wait_recv()
+            out[...] += got[d - 1].astype(jnp.float32)
 
 
 def key_call(n, first, second):
@@ -348,6 +353,58 @@
     )(*[term for row in parts for term in row], after)
 
 
+def spread_kernel(terms, *refs):
+    out, held, x_send, x_recv, c_send, c_recv = refs[terms + 1 :]
+    me = lax.axis_index("dp")
+    core = lax.rem(me, 2)
+    chip = me // 2
+    wide = held.shape[2]
+    total = refs[0][...].astype(jnp.float32)
+    for k in range(1, terms):
+        total = total + refs[k][...].astype(jnp.float32)
+    held[0] = total.astype(jnp.bfloat16)
+    across = {"dp": (1 - chip) * 2 + core}
+    beside = {"dp": chip * 2 + (1 - core)}
+    enter([across, beside])
+
+    def move(source, slot, send, recv, target):
+        copy = pltpu.make_async_remote_copy(
+            src_ref=held.at[source], dst_ref=held.at[slot], send_sem=send, recv_sem=recv,
+            device_id=target, device_id_type=MESH)
+        copy.start()
+        return copy
+
+    def place(slot, at):
+        out[:, pl.ds(pl.multiple_of(at * wide, 128), wide)] = held[slot].astype(jnp.float32)
+
+    over = move(0, 1, x_send, x_recv, across)
+    near = move(0, 2, c_send.at[0], c_recv.at[0], beside)
+    place(0, core * 2 + chip)
+    near.wait()
+    place(2, (1 - core) * 2 + chip)
+    over.wait()
+    far = move(1, 3, c_send.at[1], c_recv.at[1], beside)
+    place(1, core * 2 + (1 - chip))
+    far.wait()
+    place(3, (1 - core) * 2 + (1 - chip))
+
+
+def spread_call(came, after):
+    rows, wide = came[0].shape
+    vm = pl.BlockSpec(memory_space=VMEM)
+    dma = pltpu.SemaphoreType.DMA
+    return pl.pallas_call(
+        functools.partial(spread_kernel, len(came)),
+        out_shape=jax.ShapeDtypeStruct((rows, 4 * wide), jnp.float32),
+        in_specs=[vm] * len(came) + [pl.BlockSpec(memory_space=pl.ANY)],
+        out_specs=vm,
+        scratch_shapes=[VMEM((4, rows, wide), jnp.bfloat16), dma, dma, dma((2,)), dma((2,))],
+        compiler_params=pltpu.CompilerParams(
+            collective_id=3, has_side_effects=True, vmem_limit_bytes=24 << 20),
+        cost_estimate=pl.CostEstimate(flops=1 << 20, bytes_accessed=6 << 20, transcendentals=0),
+    )(*came, after)
+
+
 CHUNKS = 2
 LINE = 4
 PAIR = 2
@@ -366,11 +423,6 @@
         out_specs=anywhere,
         input_output_aliases={0: 0},
     )(held, *after)
-
-
-def pair_terms(away, kept, n):
-    came = lax.ppermute(away, "ctx", [(i, i ^ 1) for i in range(n)])
-    return (kept.astype(jnp.float32) + came.astype(jnp.float32)).astype(jnp.bfloat16)
 
 
 def line_terms(pair, n):
@@ -383,8 +435,6 @@
 
 
 def in_route_order(values_t, n):
-    if n != LINE * PAIR:
-        return values_t
     me = lax.axis_index("ctx")
     width, span = values_t.shape
     blocks = values_t.reshape(LINE, PAIR, width // n, span)
@@ -408,42 +458,59 @@
     half_rows = lax.dynamic_slice_in_dim(value_weight, core * half * vdim, half * vdim, 1)
     half_rows, weight = lax.optimization_barrier((half_rows, weight))
     own_weight = lax.all_gather(half_rows, "ctx", axis=0, tiled=True)
-    values_t = in_route_order(keys[:, :LAT].T, n)
+    routed = n == LINE * PAIR and m == 4
+    values_t = keys[:, :LAT].T
+    if routed:
+        values_t = in_route_order(values_t, n)
     q = jnp.transpose(query[0], (1, 2, 0))
     grad = jnp.transpose(out_grad[0], (1, 0, 2))
-    own_at = [((core * half + j * quarter) // HB).astype(jnp.int32).reshape(1) for j in range(CHUNKS)]
-    other_at = [(((1 - core) * half + j * quarter) // HB).astype(jnp.int32).reshape(1)
-                for j in range(CHUNKS)]
-    other_prob, own_prob, arrived, sums = [], [], [], []
+    chip = lax.axis_index("dp") // 2 if routed else 1
+    order = [1 - chip, chip] if routed else list(range(CHUNKS))
+
+    def place(side, part):
+        return jnp.asarray((side * half + part * quarter) // HB, jnp.int32).reshape(1)
+
+    own_at = [place(core, part) for part in order]
+    other_at = [place(1 - core, part) for part in order]
+    other_prob, own_prob, arrived, terms = [], [], [], []
     for j in range(CHUNKS):
         prob, term = forward_call(other_at[j], quarter, q, grad, keys, values_t, bias, weight)
         other_prob.append(prob)
         arrived.append(lax.ppermute(term, "dp", swap))
-    routed = n == LINE * PAIR
     for j in range(CHUNKS):
-        prob, away, kept = forward_call(
+        prob, term = forward_call(
             own_at[j], quarter, q, grad, keys, values_t, bias, weight, arrived[j])
         own_prob.append(prob)
-        if routed:
-            sums.append(pair_terms(away, kept, n))
-        else:
-            sums.append([lax.psum_scatter(
-                jnp.concatenate([away, kept], axis=0), "ctx", scatter_dimension=0, tiled=True)])
+        terms.append(term)
+    waits = [[], [], [], []]
+    if routed:
+        crossed = lax.ppermute(terms[0], "dp", [(i, i ^ 2) for i in range(m)])
+        total = terms[1].astype(jnp.float32) + crossed.astype(jnp.float32)
+        middle = total.shape[0] // 2
+        away = total[:middle].astype(jnp.bfloat16)
+        came = lax.ppermute(away, "ctx", [(i, i ^ 1) for i in range(n)])
+        pair = (total[middle:] + came.astype(jnp.float32)).astype(jnp.bfloat16)
+        lines = line_terms(pair, n)
+        waits = [[away], [], [], [pair]]
+    else:
+        shards = [[lax.psum_scatter(term, "ctx", scatter_dimension=0, tiled=True)] for term in terms]
     own_weight = held_until(own_weight, own_prob[-1])
     other_weight = lax.ppermute(own_weight, "dp", swap)
     pieces = []
-    for at, weights, probs in ((own_at, own_weight, own_prob), (other_at, other_weight, other_prob)):
+    for side, weights, probs in ((core, own_weight, own_prob), (1 - core, other_weight, other_prob)):
         for j in range(CHUNKS):
-            after = pieces[-1:]
-            if routed and weights is own_weight:
-                after = after + [sums[j]]
-                sums[j] = line_terms(sums[j], n)
+            at = jnp.concatenate(
+                [place(side, order[j]), jnp.asarray(order[j] * quarter // HB, jnp.int32).reshape(1)])
             pieces.append(backward_call(
-                at[j], j * quarter // HB, quarter, q, grad, weights, probs[j], keys, weight, after))
-    first = sum(pieces[1 : len(pieces) // 2], pieces[0])
-    second = sum(pieces[len(pieces) // 2 + 1 :], pieces[len(pieces) // 2])
+                at, quarter, q, grad, weights, probs[j], keys, weight,
+                pieces[-1:] + waits[len(pieces)]))
+    first = pieces[0] + pieces[1]
+    second = pieces[2] + pieces[3]
     latent_grad = key_call(n, first, second)
-    weight_grad = finish_call(m, sums, latent_grad)
+    if routed:
+        weight_grad = spread_call(lines, latent_grad)
+    else:
+        weight_grad = finish_call(m, shards, latent_grad)
     return (latent_grad[None], weight_grad)
 
 

time: 237 us -> 219 us (0.924)
  waiting for transfers between devices: 75.7 us -> 56.9 us
  local copies, waits for them, and re-layouts: 17 us -> 20.3 us
  Pallas kernels: 113 us -> 110 us
  other arithmetic: 2.52 us -> 5.04 us
    all_gather x1, waiting for transfers between devices: 41.5 us -> 31.8 us  [per_device(): own_weight = lax.all_gather(half_rows, 'ctx', axis=0, tiled=True)]
    ppermute x2, waiting for transfers between devices: 34.1 us -> 25.1 us  [the longest x1 23 us: per_device(): came = lax.ppermute(away, 'ctx', [(i, i ^ 1) for i in range(n)])]
    pallas_call x1, Pallas kernels: 16.6 us -> 13.3 us  [key_call(): pl.pallas_call(functools.partial(key_kernel, n), out_shape=jax.ShapeDtype...]
    unnamed x30 -> x32, local copies, waits for them, and re-layouts: 15.7 us -> 18.9 us
    ppermute x6 -> x3, starting transfers between devices: 7.45 us -> 7.01 us  [line_terms(): came.append(lax.ppermute(pair[d * rows:(d + 1) * rows], 'ctx', path))]
  transfers between devices with their start and end apart: 12 -> 9, of which waited for: 3 -> 3; matrix products, arithmetic and copies ran while one was open for 3% -> 4% of each run, Pallas kernels for 34% -> 37%
where the time goes in v2:
time: 219 us
  Pallas kernels  110 us (50%)
  waiting for transfers between devices  56.9 us (26%)
  local copies, waits for them, and re-layouts  20.3 us (9%)
  between operations  14.4 us (7%)
  starting transfers between devices  11.8 us (5%)
  other arithmetic  5.04 us (2%)
    pallas_call x4, Pallas kernels, backward_call(): pl.pallas_call(backward_kernel, grid_spec=pltpu.PrefetchScalarGridSpec(nu...  35.9 us
    all_gather x1, waiting for transfers between devices, per_device(): own_weight = lax.all_gather(half_rows, 'ctx', axis=0, tiled=True)  31.8 us
    pallas_call x4, Pallas kernels, forward_call(): pl.pallas_call(functools.partial(forward_kernel, partner is not None), gr...  30.8 us
    ppermute x1, waiting for transfers between devices, per_device(): came = lax.ppermute(away, 'ctx', [(i, i ^ 1) for i in range(n)])  23 us
    unnamed x32, local copies, waits for them, and re-layouts  18.9 us
    pallas_call x1, Pallas kernels, spread_call(): pl.pallas_call(functools.partial(spread_kernel, len(came)), out_shape=jax...  15.8 us
    pallas_call x1, Pallas kernels, start_call(): pl.pallas_call(functools.partial(start_kernel, n, lengths.shape[1]), out_...  14.6 us
    pallas_call x1, Pallas kernels, key_call(): pl.pallas_call(functools.partial(key_kernel, n), out_shape=jax.ShapeDtype...  13.3 us
  transfers between devices with their start and end apart: 9, of which 3 were waited for; matrix products, arithmetic and copies ran while one was open for 4% of the time, Pallas kernels for 37%

profile of v2, /device:TPU:5, one launch (start us, length us, event | category | flops | bytes accessed | tf_op | source)
XLA Modules:
  0.0 218.9 jit_solution(15413970705159112080)
XLA Ops:
  7.2 0.0 copy-start
  7.2 0.0 all-gather.2.cloned.1.call-start
  7.2 1.1 copy.17
  8.4 0.1 copy-done
  8.5 0.9 constant_dynamic-slice_fusion
  9.3 0.7 copy-done.9
  10.0 0.7 copy-done.10
  10.6 0.7 copy-done.11
  11.3 0.7 copy-done.12
  11.9 14.6 %shard_map.95 = (bf16[512,576]{1,0:T(8,128)(2,1)S(1)}, f32[512,128]{1,0:T(8,128)S(1)}, f32[128,128]{1,0:T(8,128)S(1)}) custom-call(s32[1,8]{1,0:T(1,128)S(1)} %copy-done.9, s32[1,8]{1,0:T(1,128)S(1)} %copy-done.10, bf16[128,576]{1,0:T(8,128)(2,1)S(1)} %bitcast.35, s32[1,128]{1,0:T(1,128)S(1)} %copy-done.11, f32[1,128]{1,0:T(1,128)S(1)} %copy-done.12), custom_call_target="tpu_custom_call" | custom-call | flops 1048576 | bytes 2097152 | tf_op jit(solution)/shard_map/pallas_call | solution.py:95
  26.5 0.0 all-gather.2.cloned.1.call-update
  26.7 0.2 copy.18
  26.9 0.2 fusion.2
  27.1 0.1 maximum_bitcast_fusion
  27.2 4.3 %copy.22 = bf16[1,128,64,128]{3,1,2,0:T(8,128)(2,1)} copy(bf16[1,128,64,128]{3,2,1,0:T(8,128)(2,1)} %param.10) | data formatting | bytes 4194304 | tf_op args[2]
  31.5 7.7 %shard_map.99 = (bf16[512,2048]{1,0:T(8,128)(2,1)S(1)}, bf16[512,2048]{1,0:T(8,128)(2,1)}) custom-call(s32[1]{0:T(128)} %bitcast.15.off, bf16[64,576,128]{2,1,0:T(8,128)(2,1)} %bitcast.36, bf16[64,128,128]{2,1,0:T(8,128)(2,1)} %bitcast.22, bf16[512,576]{1,0:T(8,128)(2,1)S(1)} %get-tuple-element.17.keys, bf16[512,512]{1,0:T(8,128)(2,1)S(1)} %bitcast.30, ...), custom_call_target="tpu_custom_call" | custom-call | flops 2550136832 | bytes 8912896 | tf_op jit(solution)/shard_map/pallas_call | solution.py:165
  39.2 1.3 copy-done.4
  40.5 1.5 collective-permute-start.1
  42.1 7.7 %shard_map.96 = (bf16[512,2048]{1,0:T(8,128)(2,1)S(1)}, bf16[512,2048]{1,0:T(8,128)(2,1)}) custom-call(s32[1]{0:T(128)} %bitcast.14.off, bf16[64,576,128]{2,1,0:T(8,128)(2,1)} %bitcast.37, bf16[64,128,128]{2,1,0:T(8,128)(2,1)} %bitcast.23, bf16[512,576]{1,0:T(8,128)(2,1)S(1)} %get-tuple-element.17.keys, bf16[512,512]{1,0:T(8,128)(2,1)S(1)} %bitcast.31, ...), custom_call_target="tpu_custom_call" | custom-call | flops 2550136832 | bytes 8912896 | tf_op jit(solution)/shard_map/pallas_call | solution.py:165
  49.8 1.3 copy-done.5
  51.1 0.0 collective-permute-start
  51.1 0.0 collective-permute-done.1.rest_0_
  51.1 8.0 %shard_map.100 = (bf16[512,2048]{1,0:T(8,128)(2,1)S(1)}, bf16[512,2048]{1,0:T(8,128)(2,1)}) custom-call(s32[1]{0:T(128)} %bitcast.off, bf16[64,576,128]{2,1,0:T(8,128)(2,1)} %bitcast.38, bf16[64,128,128]{2,1,0:T(8,128)(2,1)} %bitcast.24, bf16[512,576]{1,0:T(8,128)(2,1)S(1)} %get-tuple-element.17.keys, bf16[512,512]{1,0:T(8,128)(2,1)S(1)} %bitcast.32, ...), custom_call_target="tpu_custom_call" | custom-call | flops 2550136832 | bytes 8912896 | tf_op jit(solution)/shard_map/pallas_call | solution.py:165
  59.1 1.3 copy-done.6
  60.4 1.2 collective-permute-start.2
  61.6 0.0 collective-permute-done.rest_0_
  61.6 7.4 %shard_map.97 = (bf16[512,2048]{1,0:T(8,128)(2,1)S(1)}, bf16[512,2048]{1,0:T(8,128)(2,1)S(1)}) custom-call(s32[1]{0:T(128)} %bitcast.7.off, bf16[64,576,128]{2,1,0:T(8,128)(2,1)} %bitcast.39, bf16[64,128,128]{2,1,0:T(8,128)(2,1)} %bitcast.25, bf16[512,576]{1,0:T(8,128)(2,1)S(1)} %get-tuple-element.17.keys, bf16[512,512]{1,0:T(8,128)(2,1)S(1)} %bitcast.33, ...), custom_call_target="tpu_custom_call" | custom-call | flops 2550136832 | bytes 8912896 | tf_op jit(solution)/shard_map/pallas_call | solution.py:165
  69.0 0.0 copy-start.3
  69.0 1.3 copy-done.3
  70.3 1.4 copy-done.7
  71.7 31.8 %all-gather.2.cloned.1.call-done.held = bf16[512,4096]{1,0:T(8,128)(2,1)} async-done(((bf16[64,4096]{1,0:T(8,128)(2,1)}), bf16[512,4096]{1,0:T(8,128)(2,1)}) %all-gather.2.cloned.1.call-update) | async-done | bytes 4194320 | tf_op jit(solution)/shard_map/all_gather | solution.py:460
  103.5 1.9 collective-permute-start.3
  105.3 2.1 collective-permute-done.2
  107.5 0.0 copy-done.8
  107.5 2.3 %convert_add_fusion = f32[512,2048]{1,0:T(8,128)S(1)} fusion(bf16[512,2048]{1,0:T(8,128)(2,1)} %collective-permute-done.2, bf16[512,2048]{1,0:T(8,128)(2,1)S(1)} %copy-done.8), kind=kLoop, calls=%fused_computation | loop fusion | flops 3145728 | bytes 8388608 | tf_op jit(solution)/shard_map/add | solution.py:488
  109.8 2.0 copy-done.13
  111.8 0.1 slice.40.rest_0_
  112.0 0.1 collective-permute-start.4
  112.1 0.1 pad_add_fusion.off
  112.2 0.1 pad_add_fusion.2.off
  112.2 0.1 pad_add_fusion.1.off
  112.3 0.1 pad_add_fusion.3.off
  112.4 23.0 %collective-permute-done.4 = bf16[256,2048]{1,0:T(8,128)(2,1)S(1)} collective-permute-done((bf16[256,2048]{1,0:T(8,128)(2,1)S(1)}, bf16[256,2048]{1,0:T(8,128)(2,1)S(1)}, u32[]{:S(2)}, u32[]{:S(2)}) %collective-permute-start.4) | collective-permute-done | bytes 1048608 | tf_op jit(solution)/shard_map/ppermute | solution.py:491
  135.4 1.9 fusion.rest_1_
  137.2 0.0 copy-start.2
  137.3 0.1 fusion.3
  137.4 3.9 %collective-permute-start.5 = (bf16[64,2048]{1,0:T(8,128)(2,1)S(1)}, bf16[64,2048]{1,0:T(8,128)(2,1)S(1)}, u32[]{:S(2)}, u32[]{:S(2)}) collective-permute-start(bf16[64,2048]{1,0:T(8,128)(2,1)S(1)} %get-tuple-element.34), channel_id=1, source_target_pairs={{0,2},{1,3},{2,4},{3,5},{4,6},{5,7},{6,0},{7,1},{8,10},{9,11},{10,... | collective-permute-start | bytes 786440 | tf_op jit(solution)/shard_map/ppermute | solution.py:433
  141.3 3.1 %collective-permute-start.6 = (bf16[64,2048]{1,0:T(8,128)(2,1)S(1)}, bf16[64,2048]{1,0:T(8,128)(2,1)S(1)}, u32[]{:S(2)}, u32[]{:S(2)}) collective-permute-start(bf16[64,2048]{1,0:T(8,128)(2,1)S(1)} %get-tuple-element.33), channel_id=1, source_target_pairs={{0,4},{1,5},{2,6},{3,7},{4,0},{5,1},{6,2},{7,3},{8,12},{9,13},{10,... | collective-permute-start | bytes 786440 | tf_op jit(solution)/shard_map/ppermute | solution.py:433
  144.3 0.0 collective-permute-start.7
  144.4 8.9 %shard_map.101.rest_0_ = f32[512,576]{1,0:T(8,128)S(1)} custom-call(s32[2]{0:T(128)S(1)} %pad_add_fusion.off, bf16[64,576,128]{2,1,0:T(8,128)(2,1)} %bitcast.40, bf16[64,128,128]{2,1,0:T(8,128)(2,1)S(1)} %bitcast.27, bf16[512,4096]{1,0:T(8,128)(2,1)} %shard_map.98.value_weight, bf16[512,2048]{1,0:T(8,128)(2,1)} %copy-done.6, ...), custom_call_target="tpu_custom_call" | custom-call | flops 3623878656 | bytes 8912896 | tf_op jit(solution)/shard_map/pallas_call | solution.py:217
  153.3 8.9 %shard_map.102.rest_0_ = f32[512,576]{1,0:T(8,128)S(1)} custom-call(s32[2]{0:T(128)S(1)} %pad_add_fusion.1.off, bf16[64,576,128]{2,1,0:T(8,128)(2,1)} %bitcast.41, bf16[64,128,128]{2,1,0:T(8,128)(2,1)S(1)} %bitcast.28, bf16[512,4096]{1,0:T(8,128)(2,1)} %shard_map.98.value_weight, bf16[512,2048]{1,0:T(8,128)(2,1)} %copy-done.3, ...), custom_call_target="tpu_custom_call" | custom-call | flops 3623878656 | bytes 8912896 | tf_op jit(solution)/shard_map/pallas_call | solution.py:217
  162.3 0.1 add.72.first
  162.4 0.0 collective-permute-done.3.value_weight
  162.4 8.9 %shard_map.103.rest_0_ = f32[512,576]{1,0:T(8,128)S(1)} custom-call(s32[2]{0:T(128)S(1)} %pad_add_fusion.2.off, bf16[64,576,128]{2,1,0:T(8,128)(2,1)} %bitcast.42, bf16[64,128,128]{2,1,0:T(8,128)(2,1)S(1)} %bitcast.29, bf16[512,4096]{1,0:T(8,128)(2,1)} %collective-permute-done.3.value_weight, bf16[512,2048]{1,0:T(8,128)(2,1)} %copy-done.4, ...), custom_call_target="tpu_custom_call" | custom-call | flops 3623878656 | bytes 8912896 | tf_op jit(solution)/shard_map/pallas_call | solution.py:217
  171.4 9.1 %shard_map.104 = f32[512,576]{1,0:T(8,128)S(1)} custom-call(s32[2]{0:T(128)S(1)} %pad_add_fusion.3.off, bf16[64,576,128]{2,1,0:T(8,128)(2,1)} %bitcast.43, bf16[64,128,128]{2,1,0:T(8,128)(2,1)} %bitcast.26, bf16[512,4096]{1,0:T(8,128)(2,1)} %collective-permute-done.3.value_weight, bf16[512,2048]{1,0:T(8,128)(2,1)} %copy-done.5, ...), custom_call_target="tpu_custom_call" | custom-call | flops 3623878656 | bytes 8912896 | tf_op jit(solution)/shard_map/pallas_call | solution.py:217
  180.5 0.1 add.74.second
  180.6 13.3 %shard_map.105.refs_4_ = f32[128,576]{1,0:T(8,128)S(1)} custom-call(f32[512,576]{1,0:T(8,128)S(1)} %add.72.first, f32[512,576]{1,0:T(8,128)S(1)} %add.74.second), custom_call_target="tpu_custom_call" | custom-call | flops 1048576 | bytes 3145728 | tf_op jit(solution)/shard_map/pallas_call | solution.py:263
  193.9 0.0 collective-permute-done.5.refs_1_
  193.9 0.0 collective-permute-done.6.refs_2_
  193.9 0.0 collective-permute-done.7.refs_3_
  194.0 15.8 %shard_map.106 = f32[64,8192]{1,0:T(8,128)S(1)} custom-call(bf16[64,2048]{1,0:T(8,128)(2,1)S(1)} %get-tuple-element.35.refs_0_, bf16[64,2048]{1,0:T(8,128)(2,1)S(1)} %collective-permute-done.5.refs_1_, bf16[64,2048]{1,0:T(8,128)(2,1)S(1)} %collective-permute-done.6.refs_2_, bf16[64,2048]{1,0:T(8,128)(2,1)S(1)} %collective-permute-done.7.refs_3_, ...), custom_call_target="tpu_custom_call" | custom-call | flops 1048576 | bytes 6291456 | tf_op jit(solution)/shard_map/pallas_call | solution.py:396
  209.8 0.0 copy-start.1
  209.8 0.9 copy.20
  210.7 1.3 copy.25
  (15 shorter events, 0.1 us)
Async XLA Ops:
  7.2 1.3 copy-start
  7.2 96.3 %all-gather.2.cloned.1.call-start = ((), (), s32[]{:S(2)}) async-start(), calls=%async_computation | async-start | bytes 4718592 | tf_op jit(solution)/shard_map/all_gather | solution.py:460
  9.3 0.7 copy-start.9
  10.0 0.7 copy-start.10
  10.6 0.7 copy-start.11
  11.3 0.7 copy-start.12
  39.2 1.3 copy-start.4
  40.5 10.6 %collective-permute-start.1 = (bf16[512,2048]{1,0:T(8,128)(2,1)}, bf16[512,2048]{1,0:T(8,128)(2,1)}, u32[]{:S(2)}, u32[]{:S(2)}) collective-permute-start(bf16[512,2048]{1,0:T(8,128)(2,1)} %get-tuple-element.22), channel_id=1, source_target_pairs={{0,8},{8,0},{16,24},{24,16},{1,9},{9,1},{17,25},{25,17},{2,10},{10... | collective-permute-start | bytes 6291464 | tf_op jit(solution)/shard_map/ppermute | solution.py:479
  49.8 1.3 copy-start.5
  51.1 10.5 %collective-permute-start = (bf16[512,2048]{1,0:T(8,128)(2,1)}, bf16[512,2048]{1,0:T(8,128)(2,1)}, u32[]{:S(2)}, u32[]{:S(2)}) collective-permute-start(bf16[512,2048]{1,0:T(8,128)(2,1)} %get-tuple-element.20), channel_id=1, source_target_pairs={{0,8},{8,0},{16,24},{24,16},{1,9},{9,1},{17,25},{25,17},{2,10},{10... | collective-permute-start | bytes 6291464 | tf_op jit(solution)/shard_map/ppermute | solution.py:479
  59.1 1.3 copy-start.6
  60.4 47.1 %collective-permute-start.2 = (bf16[512,2048]{1,0:T(8,128)(2,1)}, bf16[512,2048]{1,0:T(8,128)(2,1)}, u32[]{:S(2)}, u32[]{:S(2)}) collective-permute-start(bf16[512,2048]{1,0:T(8,128)(2,1)} %get-tuple-element.25), channel_id=1, source_target_pairs={{0,16},{8,24},{16,0},{24,8},{1,17},{9,25},{17,1},{25,9},{2,18},{10... | collective-permute-start | bytes 6291464 | tf_op jit(solution)/shard_map/ppermute | solution.py:487
  69.0 1.3 copy-start.3
  70.3 1.4 copy-start.7
  103.5 4.0 %copy-start.8 = (bf16[512,2048]{1,0:T(8,128)(2,1)S(1)}, bf16[512,2048]{1,0:T(8,128)(2,1)}, u32[]{:S(2)}) copy-start(bf16[512,2048]{1,0:T(8,128)(2,1)} %copy-done.7) | copy-start | bytes 6291460
  103.5 58.9 %collective-permute-start.3 = (bf16[512,4096]{1,0:T(8,128)(2,1)}, bf16[512,4096]{1,0:T(8,128)(2,1)}, u32[]{:S(2)}, u32[]{:S(2)}) collective-permute-start(bf16[512,4096]{1,0:T(8,128)(2,1)} %shard_map.98.value_weight), channel_id=1, source_target_pairs={{0,8},{8,0},{16,24},{24,16},{1,9},{9,1},{17,25},{25,17},{2,10},{10... | collective-permute-start | bytes 12582920 | tf_op jit(solution)/shard_map/ppermute | solution.py:498
  109.8 2.0 copy-start.13
  112.0 23.4 %collective-permute-start.4 = (bf16[256,2048]{1,0:T(8,128)(2,1)S(1)}, bf16[256,2048]{1,0:T(8,128)(2,1)S(1)}, u32[]{:S(2)}, u32[]{:S(2)}) collective-permute-start(bf16[256,2048]{1,0:T(8,128)(2,1)S(1)} %slice.40.rest_0_), channel_id=1, source_target_pairs={{0,1},{1,0},{2,3},{3,2},{4,5},{5,4},{6,7},{7,6},{8,9},{9,8},{10,11... | collective-permute-start | bytes 3145736 | tf_op jit(solution)/shard_map/ppermute | solution.py:491
  137.2 7.1 %copy-start.2 = (bf16[1,128,64,128]{3,1,2,0:T(8,128)(2,1)S(1)}, bf16[1,128,64,128]{3,1,2,0:T(8,128)(2,1)}, u32[]{:S(2)}) copy-start(bf16[1,128,64,128]{3,1,2,0:T(8,128)(2,1)} %copy.22) | copy-start | bytes 6291460
  137.4 56.6 %collective-permute-start.5 = (bf16[64,2048]{1,0:T(8,128)(2,1)S(1)}, bf16[64,2048]{1,0:T(8,128)(2,1)S(1)}, u32[]{:S(2)}, u32[]{:S(2)}) collective-permute-start(bf16[64,2048]{1,0:T(8,128)(2,1)S(1)} %get-tuple-element.34), channel_id=1, source_target_pairs={{0,2},{1,3},{2,4},{3,5},{4,6},{5,7},{6,0},{7,1},{8,10},{9,11},{10,... | collective-permute-start | bytes 786440 | tf_op jit(solution)/shard_map/ppermute | solution.py:433
  141.3 52.7 %collective-permute-start.6 = (bf16[64,2048]{1,0:T(8,128)(2,1)S(1)}, bf16[64,2048]{1,0:T(8,128)(2,1)S(1)}, u32[]{:S(2)}, u32[]{:S(2)}) collective-permute-start(bf16[64,2048]{1,0:T(8,128)(2,1)S(1)} %get-tuple-element.33), channel_id=1, source_target_pairs={{0,4},{1,5},{2,6},{3,7},{4,0},{5,1},{6,2},{7,3},{8,12},{9,13},{10,... | collective-permute-start | bytes 786440 | tf_op jit(solution)/shard_map/ppermute | solution.py:433
  144.3 49.6 %collective-permute-start.7 = (bf16[64,2048]{1,0:T(8,128)(2,1)S(1)}, bf16[64,2048]{1,0:T(8,128)(2,1)S(1)}, u32[]{:S(2)}, u32[]{:S(2)}) collective-permute-start(bf16[64,2048]{1,0:T(8,128)(2,1)S(1)} %get-tuple-element.32), channel_id=1, source_target_pairs={{0,6},{1,7},{2,0},{3,1},{4,2},{5,3},{6,4},{7,5},{8,14},{9,15},{10,... | collective-permute-start | bytes 786440 | tf_op jit(solution)/shard_map/ppermute | solution.py:433
  209.8 2.2 %copy-start.1 = (bf16[64,8192]{1,0:T(8,128)(2,1)S(1)}, bf16[64,8192]{1,0:T(8,128)(2,1)}, u32[]{:S(2)}) copy-start(bf16[64,8192]{1,0:T(8,128)(2,1)} %param.11) | copy-start | bytes 3145732
Sparse Core Ops, SparseCore 0:
  26.7 76.7 all-gather.1

commit v3 on v2

--- a/solution.py
+++ b/solution.py
@@ -125,9 +125,8 @@
 
 def forward_kernel(with_sum, off, query, grad, keys, values_t, bias, weight, *rest):
     if with_sum:
-        partner, prob_ref, term_ref = rest
-    else:
-        prob_ref, term_ref = rest
+        partner = rest[0]
+    prob_ref, term_ref = rest[-2:]
     rows = query.shape[2]
     q = jnp.concatenate([query[h] for h in range(HB)], axis=1)
     score = nn(keys[...], q) * (score_scale * LOG2E) + jnp.concatenate([bias[...]] * HB, axis=1)
@@ -146,7 +145,7 @@
         term_ref[:, part] = term.astype(jnp.bfloat16)
 
 
-def forward_call(off, heads, query, grad, keys, values_t, bias, weight, partner=None):
+def forward_call(off, heads, query, grad, keys, values_t, bias, weight, partner=None, after=()):
     width, rows = query.shape[1:]
     vdim = grad.shape[2]
     span = keys.shape[0]
@@ -161,6 +160,8 @@
     if partner is not None:
         in_specs.append(column(LAT, HB * vdim))
         args.append(partner)
+    in_specs += [pl.BlockSpec(memory_space=pl.ANY)] * len(after)
+    args += after
     flops = 2 * heads * rows * (span * (width + LAT) + LAT * vdim)
     return pl.pallas_call(
         functools.partial(forward_kernel, partner is not None),
@@ -353,16 +354,18 @@
     )(*[term for row in parts for term in row], after)
 
 
-def spread_kernel(terms, *refs):
-    out, held, x_send, x_recv, c_send, c_recv = refs[terms + 1 :]
+def spread_kernel(terms, parts, *refs):
+    out, held, x_send, x_recv, c_send, c_recv = refs[terms * parts + 1 :]
     me = lax.axis_index("dp")
     core = lax.rem(me, 2)
     chip = me // 2
     wide = held.shape[2]
-    total = refs[0][...].astype(jnp.float32)
-    for k in range(1, terms):
-        total = total + refs[k][...].astype(jnp.float32)
-    held[0] = total.astype(jnp.bfloat16)
+    slim = wide // parts
+    for j in range(parts):
+        total = refs[j * terms][...].astype(jnp.float32)
+        for k in range(1, terms):
+            total = total + refs[j * terms + k][...].astype(jnp.float32)
+        held[0, :, j * slim : (j + 1) * slim] = total.astype(jnp.bfloat16)
     across = {"dp": (1 - chip) * 2 + core}
     beside = {"dp": chip * 2 + (1 - core)}
     enter([across, beside])
@@ -389,12 +392,13 @@
     place(3, (1 - core) * 2 + (1 - chip))
 
 
-def spread_call(came, after):
-    rows, wide = came[0].shape
+def spread_call(came, parts, after):
+    rows, slim = came[0].shape
+    wide = slim * parts
     vm = pl.BlockSpec(memory_space=VMEM)
     dma = pltpu.SemaphoreType.DMA
     return pl.pallas_call(
-        functools.partial(spread_kernel, len(came)),
+        functools.partial(spread_kernel, len(came) // parts, parts),
         out_shape=jax.ShapeDtypeStruct((rows, 4 * wide), jnp.float32),
         in_specs=[vm] * len(came) + [pl.BlockSpec(memory_space=pl.ANY)],
         out_specs=vm,
@@ -426,12 +430,55 @@
 
 
 def line_terms(pair, n):
-    rows = pair.shape[0] // LINE
-    came = [pair[:rows]]
+    came = [pair[0]]
     for d in range(1, LINE):
         path = [(i, (i // PAIR + d) % LINE * PAIR + i % PAIR) for i in range(n)]
-        came.append(lax.ppermute(pair[d * rows : (d + 1) * rows], "ctx", path))
+        came.append(lax.ppermute(pair[d], "ctx", path))
     return came
+
+
+def cross_kernel(term, crossed, *rest):
+    away, kept = rest[-2:]
+    total = (term[...].astype(jnp.float32) + crossed[...].astype(jnp.float32)).astype(jnp.bfloat16)
+    middle = away.shape[0]
+    away[...] = total[:middle]
+    kept[...] = total[middle:]
+
+
+def cross_call(term, crossed, part, after):
+    rows, wide = crossed.shape
+    half = jax.ShapeDtypeStruct((rows // 2, wide), jnp.bfloat16)
+    return pl.pallas_call(
+        cross_kernel,
+        grid=(1,),
+        out_shape=[half, half],
+        in_specs=[
+            pl.BlockSpec((rows, wide), lambda i: (0, part)),
+            pl.BlockSpec((rows, wide), lambda i: (0, 0)),
+        ] + [pl.BlockSpec(memory_space=pl.ANY)] * len(after),
+        out_specs=[pl.BlockSpec((rows // 2, wide), lambda i: (0, 0))] * 2,
+        compiler_params=pltpu.CompilerParams(vmem_limit_bytes=24 << 20),
+    )(term, crossed, *after)
+
+
+def pair_kernel(kept, came, after, *outs):
+    total = (kept[...].astype(jnp.float32) + came[...].astype(jnp.float32)).astype(jnp.bfloat16)
+    rows = outs[0].shape[0]
+    for d in range(LINE):
+        outs[d][...] = total[d * rows : (d + 1) * rows]
+
+
+def pair_call(kept, came, after):
+    rows, wide = kept.shape
+    block = lambda height: pl.BlockSpec((height, wide), lambda i: (0, 0))
+    return pl.pallas_call(
+        pair_kernel,
+        grid=(1,),
+        out_shape=[jax.ShapeDtypeStruct((rows // LINE, wide), jnp.bfloat16)] * LINE,
+        in_specs=[block(rows), block(rows), pl.BlockSpec(memory_space=pl.ANY)],
+        out_specs=[block(rows // LINE)] * LINE,
+        compiler_params=pltpu.CompilerParams(vmem_limit_bytes=24 << 20),
+    )(kept, came, after)
 
 
 def in_route_order(values_t, n):
@@ -479,36 +526,42 @@
         arrived.append(lax.ppermute(term, "dp", swap))
     for j in range(CHUNKS):
         prob, term = forward_call(
-            own_at[j], quarter, q, grad, keys, values_t, bias, weight, arrived[j])
+            own_at[j], quarter, q, grad, keys, values_t, bias, weight, arrived[j], own_prob[:])
         own_prob.append(prob)
         terms.append(term)
-    waits = [[], [], [], []]
     if routed:
-        crossed = lax.ppermute(terms[0], "dp", [(i, i ^ 2) for i in range(m)])
-        total = terms[1].astype(jnp.float32) + crossed.astype(jnp.float32)
-        middle = total.shape[0] // 2
-        away = total[:middle].astype(jnp.bfloat16)
-        came = lax.ppermute(away, "ctx", [(i, i ^ 1) for i in range(n)])
-        pair = (total[middle:] + came.astype(jnp.float32)).astype(jnp.bfloat16)
-        lines = line_terms(pair, n)
-        waits = [[away], [], [], [pair]]
+        wide = terms[0].shape[1] // 2
+        crossed = [lax.ppermute(
+            terms[0][:, part * wide : (part + 1) * wide], "dp", [(i, i ^ 2) for i in range(m)])
+            for part in range(2)]
+        kepts, cames = [], []
     else:
         shards = [[lax.psum_scatter(term, "ctx", scatter_dimension=0, tiled=True)] for term in terms]
-    own_weight = held_until(own_weight, own_prob[-1])
+    own_weight = held_until(own_weight, *own_prob)
     other_weight = lax.ppermute(own_weight, "dp", swap)
-    pieces = []
+    pieces, lines = [], []
     for side, weights, probs in ((core, own_weight, own_prob), (1 - core, other_weight, other_prob)):
         for j in range(CHUNKS):
             at = jnp.concatenate(
                 [place(side, order[j]), jnp.asarray(order[j] * quarter // HB, jnp.int32).reshape(1)])
+            after = pieces[-1:]
+            if routed and len(pieces) < 2:
+                part = len(pieces)
+                away, kept = cross_call(terms[1], crossed[part], part, pieces[-1:])
+                kepts.append(kept)
+                cames.append(lax.ppermute(away, "ctx", [(i, i ^ 1) for i in range(n)]))
+                after = after + [away]
+            if routed and 1 <= len(pieces) <= 2:
+                pair = pair_call(kepts[len(pieces) - 1], cames[len(pieces) - 1], pieces[-1])
+                lines = lines + line_terms(pair, n)
+                after = after + [pair[0]]
             pieces.append(backward_call(
-                at, quarter, q, grad, weights, probs[j], keys, weight,
-                pieces[-1:] + waits[len(pieces)]))
+                at, quarter, q, grad, weights, probs[j], keys, weight, after))
     first = pieces[0] + pieces[1]
     second = pieces[2] + pieces[3]
     latent_grad = key_call(n, first, second)
     if routed:
-        weight_grad = spread_call(lines, latent_grad)
+        weight_grad = spread_call(lines, 2, latent_grad)
     else:
         weight_grad = finish_call(m, shards, latent_grad)
     return (latent_grad[None], weight_grad)

time: 219 us -> 232 us (1.059)
  waiting for transfers between devices: 56.9 us -> 63.4 us
  Pallas kernels: 110 us -> 115 us
  other arithmetic: 5.04 us -> 0.89 us
  starting transfers between devices: 11.8 us -> 15.5 us
  local copies, waits for them, and re-layouts: 20.3 us -> 22.7 us
    pallas_call x1 -> x5, Pallas kernels: 15.8 us -> 22.1 us  [the longest x1 17.5 us: spread_call(): pl.pallas_call(functools.partial(spread_kernel, len(came) // parts, parts...]
    ppermute x5 -> x10, waiting for transfers between devices: 25.1 us -> 30.9 us  [the longest x2 30.9 us: per_device(): lax.ppermute(terms[0][:, part * wide:(part + 1) * wide], 'dp', [(i, i ^ 2...]
    ppermute x5 -> x10, starting transfers between devices: 8.29 us -> 12 us  [the longest x6 8.09 us: line_terms(): came.append(lax.ppermute(pair[d], 'ctx', path))]
    add x1 -> x0, other arithmetic: 2.34 us -> none  [per_device(): total = terms[1].astype(jnp.float32) + crossed.astype(jnp.float32)]
    unnamed x32 -> x36, local copies, waits for them, and re-layouts: 18.9 us -> 19.9 us
  transfers between devices with their start and end apart: 9 -> 14, of which waited for: 3 -> 3; matrix products, arithmetic and copies ran while one was open for 4% -> 3% of each run, Pallas kernels for 37% -> 36%
where the time goes in v3:
time: 232 us
  Pallas kernels  115 us (50%)
  waiting for transfers between devices  63.4 us (27%)
  local copies, waits for them, and re-layouts  22.7 us (10%)
  starting transfers between devices  15.5 us (7%)
  between operations  14.3 us (6%)
    pallas_call x4, Pallas kernels, backward_call(): pl.pallas_call(backward_kernel, grid_spec=pltpu.PrefetchScalarGridSpec(nu...  35.9 us
    all_gather x1, waiting for transfers between devices, per_device(): own_weight = lax.all_gather(half_rows, 'ctx', axis=0, tiled=True)  32.4 us
    ppermute x2, waiting for transfers between devices, per_device(): lax.ppermute(terms[0][:, part * wide:(part + 1) * wide], 'dp', [(i, i ^ 2...  30.9 us
    pallas_call x4, Pallas kernels, forward_call(): pl.pallas_call(functools.partial(forward_kernel, partner is not None), gr...  29.9 us
    unnamed x36, local copies, waits for them, and re-layouts  19.9 us
    pallas_call x1, Pallas kernels, spread_call(): pl.pallas_call(functools.partial(spread_kernel, len(came) // parts, parts...  17.5 us
    pallas_call x1, Pallas kernels, start_call(): pl.pallas_call(functools.partial(start_kernel, n, lengths.shape[1]), out_...  14.6 us
    pallas_call x1, Pallas kernels, key_call(): pl.pallas_call(functools.partial(key_kernel, n), out_shape=jax.ShapeDtype...  12.5 us
  transfers between devices with their start and end apart: 14, of which 3 were waited for; matrix products, arithmetic and copies ran while one was open for 3% of the time, Pallas kernels for 36%

profile of v3, /device:TPU:5, one launch (start us, length us, event | category | flops | bytes accessed | tf_op | source)
XLA Modules:
  0.0 231.8 jit_solution(6567215949631503364)
XLA Ops:
  7.2 0.0 copy-start
  7.2 0.0 all-gather.2.cloned.1.call-start
  7.2 1.1 copy.17
  8.4 0.1 copy-done
  8.5 0.8 constant_dynamic-slice_fusion
  9.3 0.7 copy-done.12
  10.0 0.7 copy-done.13
  10.6 0.7 copy-done.14
  11.3 0.7 copy-done.15
  11.9 14.6 %shard_map.95 = (bf16[512,576]{1,0:T(8,128)(2,1)S(1)}, f32[512,128]{1,0:T(8,128)S(1)}, f32[128,128]{1,0:T(8,128)S(1)}) custom-call(s32[1,8]{1,0:T(1,128)S(1)} %copy-done.12, s32[1,8]{1,0:T(1,128)S(1)} %copy-done.13, bf16[128,576]{1,0:T(8,128)(2,1)S(1)} %bitcast.35, s32[1,128]{1,0:T(1,128)S(1)} %copy-done.14, f32[1,128]{1,0:T(1,128)S(1)} %copy-done.15), custom_call_target="tpu_custom_call" | custom-call | flops 1048576 | bytes 2097152 | tf_op jit(solution)/shard_map/pallas_call | solution.py:95
  26.5 0.0 all-gather.2.cloned.1.call-update
  26.6 0.2 copy.18
  26.9 0.2 fusion.1
  27.1 0.1 maximum_bitcast_fusion
  27.2 4.3 %copy.22 = bf16[1,128,64,128]{3,1,2,0:T(8,128)(2,1)} copy(bf16[1,128,64,128]{3,2,1,0:T(8,128)(2,1)} %param.10) | data formatting | bytes 4194304 | tf_op args[2]
  31.4 7.7 %shard_map.96 = (bf16[512,2048]{1,0:T(8,128)(2,1)S(1)}, bf16[512,2048]{1,0:T(8,128)(2,1)}) custom-call(s32[1]{0:T(128)} %bitcast.13.off, bf16[64,576,128]{2,1,0:T(8,128)(2,1)} %bitcast.36, bf16[64,128,128]{2,1,0:T(8,128)(2,1)} %bitcast.22, bf16[512,576]{1,0:T(8,128)(2,1)S(1)} %get-tuple-element.29.keys, bf16[512,512]{1,0:T(8,128)(2,1)S(1)} %bitcast.30, ...), custom_call_target="tpu_custom_call" | custom-call | flops 2550136832 | bytes 8912896 | tf_op jit(solution)/shard_map/pallas_call | solution.py:166
  39.2 1.4 copy-done.8
  40.5 1.5 collective-permute-start
  42.1 7.7 %shard_map.98 = (bf16[512,2048]{1,0:T(8,128)(2,1)S(1)}, bf16[512,2048]{1,0:T(8,128)(2,1)}) custom-call(s32[1]{0:T(128)} %bitcast.15.off, bf16[64,576,128]{2,1,0:T(8,128)(2,1)} %bitcast.37, bf16[64,128,128]{2,1,0:T(8,128)(2,1)} %bitcast.23, bf16[512,576]{1,0:T(8,128)(2,1)S(1)} %get-tuple-element.29.keys, bf16[512,512]{1,0:T(8,128)(2,1)S(1)} %bitcast.31, ...), custom_call_target="tpu_custom_call" | custom-call | flops 2550136832 | bytes 8912896 | tf_op jit(solution)/shard_map/pallas_call | solution.py:166
  49.8 1.4 copy-done.9
  51.1 0.0 collective-permute-start.1
  51.2 7.3 %shard_map.97 = (bf16[512,2048]{1,0:T(8,128)(2,1)S(1)}, bf16[512,2048]{1,0:T(8,128)(2,1)S(1)}) custom-call(s32[1]{0:T(128)} %bitcast.off, bf16[64,576,128]{2,1,0:T(8,128)(2,1)} %bitcast.38, bf16[64,128,128]{2,1,0:T(8,128)(2,1)} %bitcast.24, bf16[512,576]{1,0:T(8,128)(2,1)S(1)} %get-tuple-element.29.keys, bf16[512,512]{1,0:T(8,128)(2,1)S(1)} %bitcast.32, ...), custom_call_target="tpu_custom_call" | custom-call | flops 2550136832 | bytes 8912896 | tf_op jit(solution)/shard_map/pallas_call | solution.py:166
  58.5 1.3 copy-done.3
  59.7 1.3 copy-done.10
  61.1 0.0 collective-permute-done.1.rest_0_
  61.1 7.2 %shard_map.99 = (bf16[512,2048]{1,0:T(8,128)(2,1)S(1)}, bf16[512,2048]{1,0:T(8,128)(2,1)S(1)}) custom-call(s32[1]{0:T(128)} %bitcast.14.off, bf16[64,576,128]{2,1,0:T(8,128)(2,1)} %bitcast.39, bf16[64,128,128]{2,1,0:T(8,128)(2,1)} %bitcast.25, bf16[512,576]{1,0:T(8,128)(2,1)S(1)} %get-tuple-element.29.keys, bf16[512,512]{1,0:T(8,128)(2,1)S(1)} %bitcast.33, ...), custom_call_target="tpu_custom_call" | custom-call | flops 2550136832 | bytes 8912896 | tf_op jit(solution)/shard_map/pallas_call | solution.py:166
  68.3 1.3 copy-done.4
  69.6 1.4 copy-done.5
  71.0 32.4 %all-gather.2.cloned.1.call-done.held = bf16[512,4096]{1,0:T(8,128)(2,1)} async-done(((bf16[64,4096]{1,0:T(8,128)(2,1)}), bf16[512,4096]{1,0:T(8,128)(2,1)}) %all-gather.2.cloned.1.call-update) | async-done | bytes 4194320 | tf_op jit(solution)/shard_map/all_gather | solution.py:507
  103.5 1.9 collective-permute-start.5
  105.3 1.6 fusion.2
  106.9 1.2 collective-permute-start.2
  108.1 0.3 collective-permute-start.3
  108.4 0.1 pad_add_fusion.off
  108.5 0.1 pad_add_fusion.2.off
  108.5 21.8 %collective-permute-done.2.crossed = bf16[512,1024]{1,0:T(8,128)(2,1)} collective-permute-done((bf16[512,1024]{1,0:T(8,128)(2,1)}, bf16[512,1024]{1,0:T(8,128)(2,1)}, u32[]{:S(2)}, u32[]{:S(2)}) %collective-permute-start.2) | collective-permute-done | bytes 1048608 | tf_op jit(solution)/shard_map/ppermute | solution.py:534
  130.3 1.6 copy-done.6
  131.9 1.5 shard_map.101
  133.4 1.2 collective-permute-start.4
  134.7 8.9 %shard_map.102.rest_0_.after = f32[512,576]{1,0:T(8,128)S(1)} custom-call(s32[2]{0:T(128)S(1)} %pad_add_fusion.off, bf16[64,576,128]{2,1,0:T(8,128)(2,1)} %bitcast.40, bf16[64,128,128]{2,1,0:T(8,128)(2,1)S(1)} %bitcast.26, bf16[512,4096]{1,0:T(8,128)(2,1)} %shard_map.100.value_weight, bf16[512,2048]{1,0:T(8,128)(2,1)} %copy-done.3, ...), custom_call_target="tpu_custom_call" | custom-call | flops 3623878656 | bytes 8912896 | tf_op jit(solution)/shard_map/pallas_call | solution.py:218
  143.6 9.1 %collective-permute-done.3.crossed = bf16[512,1024]{1,0:T(8,128)(2,1)} collective-permute-done((bf16[512,1024]{1,0:T(8,128)(2,1)}, bf16[512,1024]{1,0:T(8,128)(2,1)}, u32[]{:S(2)}, u32[]{:S(2)}) %collective-permute-start.3) | collective-permute-done | bytes 1048608 | tf_op jit(solution)/shard_map/ppermute | solution.py:534
  152.8 1.5 shard_map.103
  154.3 1.2 collective-permute-start.6
  155.6 0.1 pad_add_fusion.1.off
  155.6 0.1 pad_add_fusion.3.off
  155.7 0.0 collective-permute-done.4.came
  155.7 0.7 shard_map.104
  156.5 9.1 %shard_map.105.after.rest_0_ = f32[512,576]{1,0:T(8,128)S(1)} custom-call(s32[2]{0:T(128)S(1)} %pad_add_fusion.1.off, bf16[64,576,128]{2,1,0:T(8,128)(2,1)} %bitcast.41, bf16[64,128,128]{2,1,0:T(8,128)(2,1)S(1)} %bitcast.27, bf16[512,4096]{1,0:T(8,128)(2,1)} %shard_map.100.value_weight, bf16[512,2048]{1,0:T(8,128)(2,1)} %copy-done.4, ...), custom_call_target="tpu_custom_call" | custom-call | flops 3623878656 | bytes 8912896 | tf_op jit(solution)/shard_map/pallas_call | solution.py:218
  165.6 0.2 add.65.first
  165.7 0.6 collective-permute-start.7
  166.4 3.3 %collective-permute-start.8 = (bf16[64,1024]{1,0:T(8,128)(2,1)}, bf16[64,1024]{1,0:T(8,128)(2,1)S(1)}, u32[]{:S(2)}, u32[]{:S(2)}) collective-permute-start(bf16[64,1024]{1,0:T(8,128)(2,1)} %get-tuple-element.47), channel_id=1, source_target_pairs={{0,4},{1,5},{2,6},{3,7},{4,0},{5,1},{6,2},{7,3},{8,12},{9,13},{10,... | collective-permute-start | bytes 393224 | tf_op jit(solution)/shard_map/ppermute | solution.py:436
  169.6 0.9 collective-permute-start.9
  170.5 0.8 shard_map.106
  171.3 0.6 collective-permute-start.10
  171.9 0.0 collective-permute-start.11
  171.9 8.9 %shard_map.107.rest_0_ = f32[512,576]{1,0:T(8,128)S(1)} custom-call(s32[2]{0:T(128)S(1)} %pad_add_fusion.2.off, bf16[64,576,128]{2,1,0:T(8,128)(2,1)} %bitcast.42, bf16[64,128,128]{2,1,0:T(8,128)(2,1)S(1)} %bitcast.28, bf16[512,4096]{1,0:T(8,128)(2,1)} %collective-permute-done.5.value_weight, bf16[512,2048]{1,0:T(8,128)(2,1)} %copy-done.8, ...), custom_call_target="tpu_custom_call" | custom-call | flops 3623878656 | bytes 8912896 | tf_op jit(solution)/shard_map/pallas_call | solution.py:218
  180.9 2.7 %collective-permute-start.12 = (bf16[64,1024]{1,0:T(8,128)(2,1)}, bf16[64,1024]{1,0:T(8,128)(2,1)}, u32[]{:S(2)}, u32[]{:S(2)}) collective-permute-start(bf16[64,1024]{1,0:T(8,128)(2,1)} %get-tuple-element.51), channel_id=1, source_target_pairs={{0,6},{1,7},{2,0},{3,1},{4,2},{5,3},{6,4},{7,5},{8,14},{9,15},{10,... | collective-permute-start | bytes 393224 | tf_op jit(solution)/shard_map/ppermute | solution.py:436
  183.6 8.9 %shard_map.108 = f32[512,576]{1,0:T(8,128)S(1)} custom-call(s32[2]{0:T(128)S(1)} %pad_add_fusion.3.off, bf16[64,576,128]{2,1,0:T(8,128)(2,1)} %bitcast.43, bf16[64,128,128]{2,1,0:T(8,128)(2,1)S(1)} %bitcast.29, bf16[512,4096]{1,0:T(8,128)(2,1)} %collective-permute-done.5.value_weight, bf16[512,2048]{1,0:T(8,128)(2,1)} %copy-done.9, ...), custom_call_target="tpu_custom_call" | custom-call | flops 3623878656 | bytes 8912896 | tf_op jit(solution)/shard_map/pallas_call | solution.py:218
  192.6 0.1 add.66.second
  192.7 12.5 %shard_map.109.refs_8_ = f32[128,576]{1,0:T(8,128)S(1)} custom-call(f32[512,576]{1,0:T(8,128)S(1)} %add.65.first, f32[512,576]{1,0:T(8,128)S(1)} %add.66.second), custom_call_target="tpu_custom_call" | custom-call | flops 1048576 | bytes 3145728 | tf_op jit(solution)/shard_map/pallas_call | solution.py:264
  205.2 0.9 copy.20
  206.1 0.0 copy-start.1
  206.1 17.5 %shard_map.110 = f32[64,8192]{1,0:T(8,128)S(1)} custom-call(bf16[64,1024]{1,0:T(8,128)(2,1)S(1)} %get-tuple-element.41.rest_2_.refs_0_, bf16[64,1024]{1,0:T(8,128)(2,1)S(1)} %collective-permute-done.7.refs_1_, bf16[64,1024]{1,0:T(8,128)(2,1)S(1)} %collective-permute-done.8.refs_2_, bf16[64,1024]{1,0:T(8,128)(2,1)S(1)} %collective-permute-done.9.refs_3_, ...), custom_call_target="tpu_custom_call" | custom-call | flops 1048576 | bytes 6291456 | tf_op jit(solution)/shard_map/pallas_call | solution.py:400
  223.6 1.3 copy.25
  (30 shorter events, 0.1 us)
Async XLA Ops:
  7.2 1.3 copy-start
  7.2 96.3 %all-gather.2.cloned.1.call-start = ((), (), s32[]{:S(2)}) async-start(), calls=%async_computation | async-start | bytes 4718592 | tf_op jit(solution)/shard_map/all_gather | solution.py:507
  9.3 0.7 copy-start.12
  10.0 0.7 copy-start.13
  10.6 0.7 copy-start.14
  11.3 0.7 copy-start.15
  39.1 1.4 copy-start.8
  40.5 10.7 %collective-permute-start = (bf16[512,2048]{1,0:T(8,128)(2,1)}, bf16[512,2048]{1,0:T(8,128)(2,1)}, u32[]{:S(2)}, u32[]{:S(2)}) collective-permute-start(bf16[512,2048]{1,0:T(8,128)(2,1)} %get-tuple-element.32), channel_id=1, source_target_pairs={{0,8},{8,0},{16,24},{24,16},{1,9},{9,1},{17,25},{25,17},{2,10},{10... | collective-permute-start | bytes 6291464 | tf_op jit(solution)/shard_map/ppermute | solution.py:526
  49.8 1.4 copy-start.9
  51.1 9.9 %collective-permute-start.1 = (bf16[512,2048]{1,0:T(8,128)(2,1)}, bf16[512,2048]{1,0:T(8,128)(2,1)}, u32[]{:S(2)}, u32[]{:S(2)}) collective-permute-start(bf16[512,2048]{1,0:T(8,128)(2,1)} %get-tuple-element.34), channel_id=1, source_target_pairs={{0,8},{8,0},{16,24},{24,16},{1,9},{9,1},{17,25},{25,17},{2,10},{10... | collective-permute-start | bytes 6291464 | tf_op jit(solution)/shard_map/ppermute | solution.py:526
  58.4 1.3 copy-start.3
  59.7 1.3 copy-start.10
  68.3 1.3 copy-start.4
  69.6 1.4 copy-start.5
  103.5 1.9 copy-start.11
  103.5 68.5 %collective-permute-start.5 = (bf16[512,4096]{1,0:T(8,128)(2,1)}, bf16[512,4096]{1,0:T(8,128)(2,1)}, u32[]{:S(2)}, u32[]{:S(2)}) collective-permute-start(bf16[512,4096]{1,0:T(8,128)(2,1)} %shard_map.100.value_weight), channel_id=1, source_target_pairs={{0,8},{8,0},{16,24},{24,16},{1,9},{9,1},{17,25},{25,17},{2,10},{10... | collective-permute-start | bytes 12582920 | tf_op jit(solution)/shard_map/ppermute | solution.py:541
  106.9 27.8 %copy-start.2 = (bf16[1,128,64,128]{3,1,2,0:T(8,128)(2,1)S(1)}, bf16[1,128,64,128]{3,1,2,0:T(8,128)(2,1)}, u32[]{:S(2)}) copy-start(bf16[1,128,64,128]{3,1,2,0:T(8,128)(2,1)} %copy.22) | copy-start | bytes 6291460
  106.9 23.4 %collective-permute-start.2 = (bf16[512,1024]{1,0:T(8,128)(2,1)}, bf16[512,1024]{1,0:T(8,128)(2,1)}, u32[]{:S(2)}, u32[]{:S(2)}) collective-permute-start(bf16[512,1024]{1,0:T(8,128)(2,1)} %get-tuple-element.57), channel_id=1, source_target_pairs={{0,16},{8,24},{16,0},{24,8},{1,17},{9,25},{17,1},{25,9},{2,18},{10... | collective-permute-start | bytes 3145736 | tf_op jit(solution)/shard_map/ppermute | solution.py:534
  108.1 44.7 %collective-permute-start.3 = (bf16[512,1024]{1,0:T(8,128)(2,1)}, bf16[512,1024]{1,0:T(8,128)(2,1)}, u32[]{:S(2)}, u32[]{:S(2)}) collective-permute-start(bf16[512,1024]{1,0:T(8,128)(2,1)} %get-tuple-element.56), channel_id=1, source_target_pairs={{0,16},{8,24},{16,0},{24,8},{1,17},{9,25},{17,1},{25,9},{2,18},{10... | collective-permute-start | bytes 3145736 | tf_op jit(solution)/shard_map/ppermute | solution.py:534
  130.3 1.6 copy-start.6
  133.4 19.4 %copy-start.7 = (bf16[512,2048]{1,0:T(8,128)(2,1)S(1)}, bf16[512,2048]{1,0:T(8,128)(2,1)}, u32[]{:S(2)}) copy-start(bf16[512,2048]{1,0:T(8,128)(2,1)} %copy-done.5) | copy-start | bytes 6291460
  133.4 22.3 %collective-permute-start.4 = (bf16[256,1024]{1,0:T(8,128)(2,1)S(1)}, bf16[256,1024]{1,0:T(8,128)(2,1)S(1)}, u32[]{:S(2)}, u32[]{:S(2)}) collective-permute-start(bf16[256,1024]{1,0:T(8,128)(2,1)S(1)} %get-tuple-element.38.rest_0_), channel_id=1, source_target_pairs={{0,1},{1,0},{2,3},{3,2},{4,5},{5,4},{6,7},{7,6},{8,9},{9,8},{10,11... | collective-permute-start | bytes 1572872 | tf_op jit(solution)/shard_map/ppermute | solution.py:552
  154.3 16.2 %collective-permute-start.6 = (bf16[256,1024]{1,0:T(8,128)(2,1)S(1)}, bf16[256,1024]{1,0:T(8,128)(2,1)S(1)}, u32[]{:S(2)}, u32[]{:S(2)}) collective-permute-start(bf16[256,1024]{1,0:T(8,128)(2,1)S(1)} %get-tuple-element.39.rest_1_), channel_id=1, source_target_pairs={{0,1},{1,0},{2,3},{3,2},{4,5},{5,4},{6,7},{7,6},{8,9},{9,8},{10,11... | collective-permute-start | bytes 1572872 | tf_op jit(solution)/shard_map/ppermute | solution.py:552
  165.7 15.1 %collective-permute-start.7 = (bf16[64,1024]{1,0:T(8,128)(2,1)S(1)}, bf16[64,1024]{1,0:T(8,128)(2,1)S(1)}, u32[]{:S(2)}, u32[]{:S(2)}) collective-permute-start(bf16[64,1024]{1,0:T(8,128)(2,1)S(1)} %get-tuple-element.46), channel_id=1, source_target_pairs={{0,2},{1,3},{2,4},{3,5},{4,6},{5,7},{6,0},{7,1},{8,10},{9,11},{10,... | collective-permute-start | bytes 393224 | tf_op jit(solution)/shard_map/ppermute | solution.py:436
  166.4 39.7 %collective-permute-start.8 = (bf16[64,1024]{1,0:T(8,128)(2,1)}, bf16[64,1024]{1,0:T(8,128)(2,1)S(1)}, u32[]{:S(2)}, u32[]{:S(2)}) collective-permute-start(bf16[64,1024]{1,0:T(8,128)(2,1)} %get-tuple-element.47), channel_id=1, source_target_pairs={{0,4},{1,5},{2,6},{3,7},{4,0},{5,1},{6,2},{7,3},{8,12},{9,13},{10,... | collective-permute-start | bytes 393224 | tf_op jit(solution)/shard_map/ppermute | solution.py:436
  169.6 36.4 %collective-permute-start.9 = (bf16[64,1024]{1,0:T(8,128)(2,1)}, bf16[64,1024]{1,0:T(8,128)(2,1)S(1)}, u32[]{:S(2)}, u32[]{:S(2)}) collective-permute-start(bf16[64,1024]{1,0:T(8,128)(2,1)} %get-tuple-element.48), channel_id=1, source_target_pairs={{0,6},{1,7},{2,0},{3,1},{4,2},{5,3},{6,4},{7,5},{8,14},{9,15},{10,... | collective-permute-start | bytes 393224 | tf_op jit(solution)/shard_map/ppermute | solution.py:436
  171.3 34.8 %collective-permute-start.10 = (bf16[64,1024]{1,0:T(8,128)(2,1)}, bf16[64,1024]{1,0:T(8,128)(2,1)}, u32[]{:S(2)}, u32[]{:S(2)}) collective-permute-start(bf16[64,1024]{1,0:T(8,128)(2,1)} %get-tuple-element.49), channel_id=1, source_target_pairs={{0,2},{1,3},{2,4},{3,5},{4,6},{5,7},{6,0},{7,1},{8,10},{9,11},{10,... | collective-permute-start | bytes 393224 | tf_op jit(solution)/shard_map/ppermute | solution.py:436
  171.9 34.2 %collective-permute-start.11 = (bf16[64,1024]{1,0:T(8,128)(2,1)}, bf16[64,1024]{1,0:T(8,128)(2,1)}, u32[]{:S(2)}, u32[]{:S(2)}) collective-permute-start(bf16[64,1024]{1,0:T(8,128)(2,1)} %get-tuple-element.50), channel_id=1, source_target_pairs={{0,4},{1,5},{2,6},{3,7},{4,0},{5,1},{6,2},{7,3},{8,12},{9,13},{10,... | collective-permute-start | bytes 393224 | tf_op jit(solution)/shard_map/ppermute | solution.py:436
  180.9 25.2 %collective-permute-start.12 = (bf16[64,1024]{1,0:T(8,128)(2,1)}, bf16[64,1024]{1,0:T(8,128)(2,1)}, u32[]{:S(2)}, u32[]{:S(2)}) collective-permute-start(bf16[64,1024]{1,0:T(8,128)(2,1)} %get-tuple-element.51), channel_id=1, source_target_pairs={{0,6},{1,7},{2,0},{3,1},{4,2},{5,3},{6,4},{7,5},{8,14},{9,15},{10,... | collective-permute-start | bytes 393224 | tf_op jit(solution)/shard_map/ppermute | solution.py:436
  206.1 18.8 %copy-start.1 = (bf16[64,8192]{1,0:T(8,128)(2,1)S(1)}, bf16[64,8192]{1,0:T(8,128)(2,1)}, u32[]{:S(2)}) copy-start(bf16[64,8192]{1,0:T(8,128)(2,1)} %param.11) | copy-start | bytes 3145732
Sparse Core Ops, SparseCore 0:
  26.6 76.7 all-gather.1
